TPU v7x, 32 devices: a whole 2x2x4 slice. The times are simulated.
32 devices in a mesh: dp: 16 (over z, y, core), seq: 2 (over x).
Axes of the slice: x: 2, y: 2, z: 4, core: 2. Of those that a mesh axis runs over, the one named last changes fastest.
Arguments:
- inputs: bfloat16 [16, 1024, 768], P('dp', 'seq'), may hold values from -6 to 6
- modality: int32 [16, 1024], P('dp'), may hold values from 0 to 2, never falling along the last dimension, each value on 1 to 512 neighbouring positions
- key_valid_mask: int32 [16, 1024], P('dp'), may hold values 0 or 1
- output_gradient: bfloat16 [16, 1024, 768], P('dp', 'seq'), may hold values from -6 to 6
- mats: float32 [768, 9216], P('dp'), may hold values from -2 to 2
- mats_momentum: float32 [768, 9216], P('dp')
- mats_average: float32 [768, 9216], P('dp'), may hold values from -2 to 2
- smalls: float32 [768, 15], P('dp'), may hold values from -2 to 2
- smalls_momentum: float32 [768, 15], P('dp')
- smalls_average: float32 [768, 15], P('dp'), may hold values from -2 to 2
Outputs:
- block_out: bfloat16 [16, 1024, 768], P('dp', 'seq')
- input_grad: bfloat16 [16, 1024, 768], P('dp', 'seq')
- mats_grad: float32 [768, 9216], P('dp')
- new_mats: float32 [768, 9216], P('dp')
- new_mats_momentum: float32 [768, 9216], P('dp')
- new_mats_average: float32 [768, 9216], P('dp')
- smalls_grad: float32 [768, 15], P('dp')
- out_bias_grad: float32 [768], P('dp')
- new_smalls: float32 [768, 15], P('dp')
- new_smalls_momentum: float32 [768, 15], P('dp')
- new_smalls_average: float32 [768, 15], P('dp')
Inputs may be any that keep to these rules, and one draw needn't show every extreme that they name: Along a document's positions the modality never falls; each of the three fills 1 to 512 positions, one of them exactly that many.
All inputs are finite; a program needn't handle non-finite values. No bound on the sum of `key_valid_mask` on one device may be relied on, other than what follows from the above.
Results may differ from a plain program's by a relative error of at most 0.019.
Values may be sent and summed in bfloat16 or wider, within the bound.
No kernel may reach another device: no remote copies, remote signals or barrier semaphores. Data moves between devices by JAX's collectives and lax.ppermute only.
A program may use at most 192 MiB of HBM per device.

v0:
```python
import math

import jax
import jax.numpy as jnp
from jax import lax
from jax.sharding import PartitionSpec as P

MODEL_WIDTH = 768
H = 12
HD = 64
FF = 3072


epsilon = 1e-06
momentum_rate = 0.9
decay_rate = 0.0001
average_rate = 0.75
base_rate = 0.03
masked_score = -1e30


def product(left, right):
    return jnp.dot(left, right, preferred_element_type=jnp.float32)


def product_tn(left, right):
    return lax.dot_general(
        left, right, (((0,), (0,)), ((), ())), preferred_element_type=jnp.float32
    )


def product_nt(left, right):
    return lax.dot_general(
        left, right, (((1,), (1,)), ((), ())), preferred_element_type=jnp.float32
    )


def normalize(rows, gain, shift):
    mean = jnp.mean(rows, axis=-1, keepdims=True)
    centred = rows - mean
    spread = jnp.mean(centred * centred, axis=-1, keepdims=True)
    return centred * lax.rsqrt(spread + epsilon) * gain + shift


def exact_gelu(values):
    return jax.nn.gelu(values, approximate=False)


def head_scores(query_heads, key_heads, live_doc):
    scores = (
        jnp.einsum("qhe,khe->hqk", query_heads, key_heads, preferred_element_type=jnp.float32)
        * 0.125
    )
    return jnp.where(live_doc[None, None, :] > 0, scores, masked_score)


def attention_forward_pass(item):
    query_doc, keys_doc, values_doc, live_doc = item
    query_heads = query_doc.reshape(query_doc.shape[0], H, HD)
    key_heads = keys_doc.reshape(keys_doc.shape[0], H, HD)
    value_heads = values_doc.reshape(values_doc.shape[0], H, HD)
    scores = head_scores(query_heads, key_heads, live_doc)
    top = jnp.max(scores, axis=-1, keepdims=True)
    expd = jnp.exp(scores - top)
    total = jnp.sum(expd, axis=-1, keepdims=True)
    prob = (expd / total).astype(jnp.bfloat16)
    attention_output = jnp.einsum(
        "hqk,khe->qhe", prob, value_heads, preferred_element_type=jnp.float32
    )
    return (attention_output.reshape(query_doc.shape[0], H * HD), (top + jnp.log(total))[..., 0])


def attention_backward_pass(item):
    query_doc, keys_doc, values_doc, live_doc, log_sum_normalizer, grad_doc = item
    element_count = query_doc.shape[0]
    length = keys_doc.shape[0]
    query_heads = query_doc.reshape(element_count, H, HD)
    key_heads = keys_doc.reshape(length, H, HD)
    value_heads = values_doc.reshape(length, H, HD)
    grad_heads = grad_doc.reshape(element_count, H, HD)
    scores = head_scores(query_heads, key_heads, live_doc)
    prob = jnp.exp(scores - log_sum_normalizer[..., None])
    grad_prob = jnp.einsum(
        "qhe,khe->hqk", grad_heads, value_heads, preferred_element_type=jnp.float32
    )
    grad_values = jnp.einsum(
        "hqk,qhe->khe", prob.astype(jnp.bfloat16), grad_heads, preferred_element_type=jnp.float32
    )
    inner = jnp.sum(prob * grad_prob, axis=-1, keepdims=True)
    grad_scores = (prob * (grad_prob - inner)).astype(jnp.bfloat16)
    grad_query = (
        jnp.einsum("hqk,khe->qhe", grad_scores, key_heads, preferred_element_type=jnp.float32)
        * 0.125
    )
    grad_keys = (
        jnp.einsum("hqk,qhe->khe", grad_scores, query_heads, preferred_element_type=jnp.float32)
        * 0.125
    )
    return (
        grad_query.reshape(element_count, H * HD),
        grad_keys.reshape(length, H * HD),
        grad_values.reshape(length, H * HD),
    )


def per_device(
    inputs,
    modality,
    key_valid_mask,
    output_gradient,
    mats,
    mats_momentum,
    mats_average,
    smalls,
    smalls_momentum,
    smalls_average,
):
    docs, local_len, width = inputs.shape
    seq_len = modality.shape[1]
    rows = docs * local_len
    low_mats = mats.astype(jnp.bfloat16)
    w_qkv, w_out, w_up, w_down, whole_smalls = (
        lax.all_gather(low_mats[:, 0 : 3 * MODEL_WIDTH], "dp", axis=0, tiled=True),
        lax.all_gather(low_mats[:, 3 * MODEL_WIDTH : 4 * MODEL_WIDTH], "dp", axis=0, tiled=True),
        lax.all_gather(
            low_mats[:, 4 * MODEL_WIDTH : 4 * MODEL_WIDTH + FF], "dp", axis=0, tiled=True
        ),
        lax.all_gather(low_mats[:, 4 * MODEL_WIDTH + FF :], "dp", axis=0, tiled=True),
        lax.all_gather(smalls.astype(jnp.bfloat16), "dp", axis=0, tiled=True),
    )
    params = whole_smalls.astype(jnp.float32)
    bias_qkv = jnp.concatenate([params[:, 0], jnp.zeros_like(params[:, 0]), params[:, 1]])
    bias_up = jnp.transpose(params[:, 8:12]).reshape(FF)
    embed = jnp.transpose(whole_smalls[:, 12:15])
    leading_key = (jnp.arange(seq_len) == 0).astype(jnp.int32)
    valid_positions = jnp.maximum(key_valid_mask, leading_key[None, :])
    local_start = lax.axis_index("seq") * local_len
    local_modality = lax.dynamic_slice_in_dim(modality, local_start, local_len, 1)
    onehot = (
        local_modality.reshape(rows)[:, None] == jnp.arange(3, dtype=jnp.int32)[None, :]
    ).astype(jnp.bfloat16)
    x_in = inputs.reshape(rows, width).astype(jnp.float32) + product(onehot, embed)
    x_low = x_in.astype(jnp.bfloat16)
    qkv = (product(x_low, w_qkv) + bias_qkv).astype(jnp.bfloat16)
    query_documents = qkv[:, 0:width].reshape(docs, local_len, width)
    keys_local = qkv[:, width : 2 * width].reshape(docs, local_len, width)
    values_local = qkv[:, 2 * width :].reshape(docs, local_len, width)
    every_key, every_value = (
        lax.all_gather(keys_local, "seq", axis=1, tiled=True),
        lax.all_gather(values_local, "seq", axis=1, tiled=True),
    )
    attention_output, log_sum_normalizer = lax.map(
        attention_forward_pass, (query_documents, every_key, every_value, valid_positions)
    )
    out_low = attention_output.reshape(rows, width).astype(jnp.bfloat16)
    mixed = product(out_low, w_out) + params[:, 2]
    first_in = x_in + mixed
    first = normalize(first_in, params[:, 4], params[:, 5])
    first_low = first.astype(jnp.bfloat16)
    up = product(first_low, w_up) + bias_up
    act_low = exact_gelu(up).astype(jnp.bfloat16)
    ffo = product_nt(act_low, w_down) + params[:, 3]
    second_in = first + ffo
    result = normalize(second_in, params[:, 6], params[:, 7])
    block_out = result.astype(jnp.bfloat16).reshape(docs, local_len, width)
    w_qkv, w_out, w_up, w_down = (
        lax.all_gather(low_mats[:, 0 : 3 * MODEL_WIDTH], "dp", axis=0, tiled=True),
        lax.all_gather(low_mats[:, 3 * MODEL_WIDTH : 4 * MODEL_WIDTH], "dp", axis=0, tiled=True),
        lax.all_gather(
            low_mats[:, 4 * MODEL_WIDTH : 4 * MODEL_WIDTH + FF], "dp", axis=0, tiled=True
        ),
        lax.all_gather(low_mats[:, 4 * MODEL_WIDTH + FF :], "dp", axis=0, tiled=True),
    )
    grad_rows = output_gradient.reshape(rows, width).astype(jnp.float32)
    second_out, second_pull = jax.vjp(normalize, second_in, params[:, 6], params[:, 7])
    grad_second, grad_gain2, grad_shift2 = second_pull(grad_rows)
    grad_ffo = grad_second.astype(jnp.bfloat16)
    grad_bias_down = jnp.sum(grad_ffo.astype(jnp.float32), axis=0)
    grad_w_down = product_tn(grad_ffo, act_low)
    grad_act = product(grad_ffo, w_down)
    gelu_out, gelu_pull = jax.vjp(exact_gelu, up)
    grad_up = gelu_pull(grad_act)[0].astype(jnp.bfloat16)
    grad_bias_up = jnp.sum(grad_up.astype(jnp.float32), axis=0)
    grad_w_up = product_tn(first_low, grad_up)
    grad_first = grad_second + product_nt(grad_up, w_up)
    first_out, first_pull = jax.vjp(normalize, first_in, params[:, 4], params[:, 5])
    grad_first_in, grad_gain1, grad_shift1 = first_pull(grad_first)
    grad_mixed = grad_first_in.astype(jnp.bfloat16)
    grad_bias_out = jnp.sum(grad_mixed.astype(jnp.float32), axis=0)
    grad_w_out = product_tn(out_low, grad_mixed)
    grad_out = product_nt(grad_mixed, w_out).astype(jnp.bfloat16)
    output_gradient_documents = grad_out.reshape(docs, local_len, width)
    grad_query, grad_keys_all, grad_values_all = lax.map(
        attention_backward_pass,
        (
            query_documents,
            every_key,
            every_value,
            valid_positions,
            log_sum_normalizer,
            output_gradient_documents,
        ),
    )
    grad_keys, grad_values = (
        lax.psum_scatter(
            grad_keys_all.astype(jnp.bfloat16), "seq", scatter_dimension=1, tiled=True
        ).astype(jnp.float32),
        lax.psum_scatter(
            grad_values_all.astype(jnp.bfloat16), "seq", scatter_dimension=1, tiled=True
        ).astype(jnp.float32),
    )
    grad_qkv = jnp.concatenate(
        [
            grad_query.reshape(rows, width).astype(jnp.bfloat16),
            grad_keys.reshape(rows, width).astype(jnp.bfloat16),
            grad_values.reshape(rows, width).astype(jnp.bfloat16),
        ],
        axis=1,
    )
    grad_bias_qkv = jnp.sum(grad_qkv.astype(jnp.float32), axis=0)
    grad_w_qkv = product_tn(x_low, grad_qkv)
    grad_x_in = grad_first_in + product_nt(grad_qkv, w_qkv)
    grad_embed = lax.dot_general(
        onehot.astype(jnp.float32),
        grad_x_in,
        (((0,), (0,)), ((), ())),
        precision=lax.Precision.HIGHEST,
        preferred_element_type=jnp.float32,
    )
    input_grad = grad_x_in.astype(jnp.bfloat16).reshape(docs, local_len, width)
    grad_columns = jnp.stack(
        [
            grad_bias_qkv[0:width],
            grad_bias_qkv[2 * width :],
            grad_bias_out,
            grad_bias_down,
            grad_gain1,
            grad_shift1,
            grad_gain2,
            grad_shift2,
        ],
        axis=1,
    )
    grad_smalls = jnp.concatenate(
        [
            grad_columns,
            jnp.transpose(grad_bias_up.reshape(FF // width, width)),
            jnp.transpose(grad_embed),
        ],
        axis=1,
    )
    qkv_shard, out_shard, up_shard, down_shard, small_shard = (
        lax.psum_scatter(
            grad_w_qkv.astype(jnp.bfloat16), "dp", scatter_dimension=0, tiled=True
        ).astype(jnp.float32),
        lax.psum_scatter(
            grad_w_out.astype(jnp.bfloat16), "dp", scatter_dimension=0, tiled=True
        ).astype(jnp.float32),
        lax.psum_scatter(
            grad_w_up.astype(jnp.bfloat16), "dp", scatter_dimension=0, tiled=True
        ).astype(jnp.float32),
        lax.psum_scatter(
            grad_w_down.astype(jnp.bfloat16), "dp", scatter_dimension=0, tiled=True
        ).astype(jnp.float32),
        lax.psum_scatter(
            grad_smalls.astype(jnp.bfloat16), "dp", scatter_dimension=0, tiled=True
        ).astype(jnp.float32),
    )
    mats_shard = jnp.concatenate([qkv_shard, out_shard, up_shard, down_shard], axis=1)
    mats_grad, smalls_grad = (
        lax.psum(mats_shard.astype(jnp.bfloat16), "seq").astype(jnp.float32),
        lax.psum(small_shard.astype(jnp.bfloat16), "seq").astype(jnp.float32),
    )
    out_bias_grad = smalls_grad[:, 2]
    total_tokens = rows * lax.axis_size("dp") * lax.axis_size("seq")
    rate = base_rate / math.sqrt(total_tokens)
    decayed = mats_grad + decay_rate * mats
    new_mats_momentum = momentum_rate * mats_momentum + decayed
    new_mats = mats - rate * (decayed + momentum_rate * new_mats_momentum)
    new_mats_average = average_rate * mats_average + (1.0 - average_rate) * new_mats
    new_smalls_momentum = momentum_rate * smalls_momentum + smalls_grad
    new_smalls = smalls - rate * (smalls_grad + momentum_rate * new_smalls_momentum)
    new_smalls_average = average_rate * smalls_average + (1.0 - average_rate) * new_smalls
    return (
        block_out,
        input_grad,
        mats_grad,
        new_mats,
        new_mats_momentum,
        new_mats_average,
        smalls_grad,
        out_bias_grad,
        new_smalls,
        new_smalls_momentum,
        new_smalls_average,
    )


def solution(mesh):
    placed = (
        P("dp", "seq", None),
        P("dp", None),
        P("dp", None),
        P("dp", "seq", None),
        P("dp", None),
        P("dp", None),
        P("dp", None),
        P("dp", None),
        P("dp", None),
        P("dp", None),
    )
    return jax.shard_map(
        per_device,
        mesh=mesh,
        in_specs=placed,
        out_specs=(
            P("dp", "seq", None),
            P("dp", "seq", None),
            P("dp", None),
            P("dp", None),
            P("dp", None),
            P("dp", None),
            P("dp", None),
            P("dp"),
            P("dp", None),
            P("dp", None),
            P("dp", None),
        ),
        check_vma=False,
    )
```

profile of v0, /device:TPU:0, one launch (start us, length us, event | category | flops | bytes accessed | tf_op | source)
XLA Modules:
  0.0 777.5 jit_solution(7473604885597649127)
XLA Ops:
  7.2 1.6 convert_element_type.179
  10.4 23.3 %all-gather.2 = bf16[16,48,15]{1,2,0:T(8,128)(2,1)S(1)} all-gather(bf16[1,48,15]{1,2,0:T(8,128)(2,1)S(1)} %convert_bitcast_fusion.1), channel_id=1, replica_groups=mesh['dp'=16,'seq'=2] {'dp'}, dimensions={0}, use_global_device_ids=true | all-gather | bytes 24480 | tf_op jit(solution)/shard_map/all_gather | solution.py:129
  34.9 25.7 %all-gather.10.cloned.1.call-done = bf16[768,2304]{1,0:T(8,128)(2,1)} async-done(((bf16[48,2304]{1,0:T(8,128)(2,1)}), bf16[768,2304]{1,0:T(8,128)(2,1)}) %all-gather.10.cloned.1.call-update) | async-done | bytes 3538960 | tf_op jit(solution)/shard_map/all_gather | solution.py:123
  60.6 4.0 fusion.13
  64.6 1.3 fusion.46
  69.6 22.7 %all-gather.20.cloned.1.call-done = bf16[1024,768]{1,0:T(8,128)(2,1)} async-done(((bf16[512,768]{1,0:T(8,128)(2,1)}), bf16[1024,768]{1,0:T(8,128)(2,1)}) %all-gather.20.cloned.1.call-update) | async-done | bytes 1572880 | tf_op jit(solution)/shard_map/all_gather | solution.py:149
  92.3 1.7 copy.37
  94.0 10.7 %fusion.6 = (f32[12,512]{1,0:T(8,128)S(1)}, f32[12,512,1024]{2,1,0:T(8,128)}) fusion(pred[1024]{0:T(1024)(128)(4,1)S(1)} %compare_reduce_fusion, bf16[512,12,64]{0,2,1:T(8,128)(2,1)S(1)} %bitcast.73, bf16[1024,12,64]{0,2,1:T(8,128)(2,1)S(1)} %bitcast.71), kind=kOutput, calls=%fused_computation.11 | convolution fusion | flops 824174592 | bytes 27550720 | tf_op jit(solution)/shard_map/while/body/eval_jaxpr/qhe,khe->hqk/dot_general | solution.py:51
  104.7 11.2 %fusion = f32[12,512]{1,0:T(8,128)S(1)} fusion(f32[12,512]{1,0:T(8,128)S(1)} %get-tuple-element.103, f32[12,512,1024]{2,1,0:T(8,128)} %get-tuple-element.104, pred[1024]{0:T(1024)(128)(4,1)S(1)} %compare_reduce_fusion), kind=kLoop, calls=%fused_computation.6 | loop fusion | flops 25159680 | bytes 25216000 | tf_op jit(solution)/shard_map/while/body/eval_jaxpr/reduce_sum | solution.py:65
  115.9 5.7 all-gather.18.cloned.1.call-done
  121.7 1.7 copy.35
  123.4 12.1 %fusion.21 = bf16[12,64,512]{2,1,0:T(8,128)(2,1)} fusion(bf16[1024,12,64]{0,2,1:T(8,128)(2,1)S(1)} %bitcast.76, f32[12,512]{1,0:T(8,128)S(1)} %fusion, f32[12,512]{1,0:T(8,128)S(1)} %get-tuple-element.103, f32[12,512,1024]{2,1,0:T(8,128)} %get-tuple-element.104, pred[1024]{0:T(1024)(128)(4,1)S(1)} %compare_reduce_fusion), kind=kOutput, calls=%fused_computation.65 | convolution fusion | flops 837156864 | bytes 27575296 | tf_op jit(solution)/shard_map/while/body/eval_jaxpr/hqk,khe->qhe/dot_general | solution.py:67
  135.5 27.3 %all-gather.12.cloned.1.call-done = bf16[768,768]{1,0:T(8,128)(2,1)} async-done(((bf16[48,768]{1,0:T(8,128)(2,1)}), bf16[768,768]{1,0:T(8,128)(2,1)}) %all-gather.12.cloned.1.call-update) | async-done | bytes 1179664 | tf_op jit(solution)/shard_map/all_gather | solution.py:124
  162.7 2.9 fusion.49
  166.0 51.8 %all-gather.14.cloned.1.call-done = bf16[768,3072]{1,0:T(8,128)(2,1)} async-done(((bf16[48,3072]{1,0:T(8,128)(2,1)}), bf16[768,3072]{1,0:T(8,128)(2,1)}) %all-gather.14.cloned.1.call-update) | async-done | bytes 4718608 | tf_op jit(solution)/shard_map/all_gather | solution.py:125
  217.8 20.1 %multiply_convert_fusion.1 = (bf16[512,3072]{1,0:T(8,128)(2,1)}, f32[512,3072]{1,0:T(8,128)}, f32[512,3072]{1,0:T(8,128)}) fusion(f32[3072]{0:T(1024)S(1)} %add.163, bf16[768,3072]{1,0:T(8,128)(2,1)} %all-gather.14.cloned.1.call-done, f32[512,768]{1,0:T(8,128)S(1)} %get-tuple-element.106, f32[768]{0:T(1024)S(1)} %get-tuple-element.70, ...), kind=kOutput, calls=%fused_computation.15 | convolution fusion | flops 2521694208 | bytes 22042624 | tf_op jit(solution)/shard_map/dot_general | solution.py:23
  237.9 34.6 %all-gather.16.cloned.1.call-done = bf16[768,3072]{1,0:T(8,128)(2,1)} async-done(((bf16[48,3072]{1,0:T(8,128)(2,1)}), bf16[768,3072]{1,0:T(8,128)(2,1)}) %all-gather.16.cloned.1.call-update) | async-done | bytes 4718608 | tf_op jit(solution)/shard_map/all_gather | solution.py:128
  272.5 6.6 fusion.50
  280.2 1.6 fusion.44
  282.0 1.9 copy-done.28
  283.9 7.0 fusion.40
  291.0 3.2 multiply_reduce_fusion.1
  294.9 1.1 copy-done.9
  297.1 1.7 convolution_convert_fusion.4
  298.8 1.4 copy.38
  300.2 12.4 %fusion.16 = bf16[12,64,1024]{2,1,0:T(8,128)(2,1)} fusion(bf16[512,12,64]{0,2,1:T(8,128)(2,1)S(1)} %bitcast.81, f32[12,512]{1,0:T(8,128)S(1)} %log_add_fusion, f32[12,512,1024]{2,1,0:T(8,128)} %get-tuple-element.104, pred[1024]{0:T(1024)(128)(4,1)S(1)} %compare_reduce_fusion), kind=kOutput, calls=%fused_computation.46 | convolution fusion | flops 831258624 | bytes 27550720 | tf_op jit(solution)/shard_map/while/body/eval_jaxpr/hqk,qhe->khe/dot_general | solution.py:86
  312.7 20.8 %multiply_reduce_fusion = (f32[12,512]{1,0:T(8,128)S(1)}, f32[12,512,1024]{2,1,0:T(8,128)}) fusion(f32[12,512]{1,0:T(8,128)S(1)} %log_add_fusion, f32[12,512,1024]{2,1,0:T(8,128)} %get-tuple-element.104, pred[1024]{0:T(1024)(128)(4,1)S(1)} %compare_reduce_fusion, bf16[512,12,64]{0,2,1:T(8,128)(2,1)S(1)} %bitcast.82, bf16[1024,12,64]{0,2,1:T(8,128)(2,1)S(1)} %bitcast.77), kind=kOutput, calls=%fused_computation.1 | convolution fusion | flops 836757504 | bytes 52741120 | tf_op jit(solution)/shard_map/while/body/eval_jaxpr/qhe,khe->hqk/dot_general | solution.py:83
  333.5 16.9 %multiply_convert_fusion = bf16[12,512,1024]{2,1,0:T(8,128)(2,1)S(1)} fusion(f32[12,512,1024]{2,1,0:T(8,128)} %get-tuple-element.112, f32[12,512]{1,0:T(8,128)S(1)} %get-tuple-element.111, f32[12,512]{1,0:T(8,128)S(1)} %log_add_fusion, f32[12,512,1024]{2,1,0:T(8,128)} %get-tuple-element.104, pred[1024]{0:T(1024)(128)(4,1)S(1)} %compare_reduce_fusion), kind=kLoop, calls=%fused_computation | loop fusion | flops 37748736 | bytes 62964736 | tf_op jit(solution)/shard_map/while/body/eval_jaxpr/convert_element_type | solution.py:90
  350.4 4.1 multiply_convert_fusion.2
  354.5 1.0 copy-done.2
  355.6 3.0 convolution_convert_fusion.3
  358.7 6.8 convolution_convert_fusion.1
  365.6 1.1 copy-done.18
  366.6 6.3 convolution_convert_fusion
  373.2 1.1 copy-done.4
  374.3 8.6 %multiply_convert_fusion.3 = bf16[12,64,512]{2,1,0:T(8,128)(2,1)S(1)} fusion(bf16[1024,12,64]{0,2,1:T(8,128)(2,1)S(1)} %bitcast.72, bf16[12,512,1024]{2,1,0:T(8,128)(2,1)} %copy-done.2), kind=kOutput, calls=%fused_computation.51 | convolution fusion | flops 806092800 | bytes 14942208 | tf_op jit(solution)/shard_map/while/body/eval_jaxpr/hqk,khe->qhe/dot_general | solution.py:92
  383.0 5.9 convolution_convert_fusion.2
  389.2 1.9 fusion.36
  391.2 4.9 add_add_fusion.4
  397.9 44.1 %reduce-scatter.16.cloned.1.call-done = bf16[48,768]{1,0:T(8,128)(2,1)} async-done(((bf16[768,768]{1,0:T(8,128)(2,1)}), bf16[48,768]{1,0:T(8,128)(2,1)}) %reduce-scatter.16.cloned.1.call-update) | async-done | bytes 73744 | tf_op jit(solution)/shard_map/reduce_scatter | solution.py:256
  442.0 78.3 %reduce-scatter.18.cloned.1.call-done = bf16[48,3072]{1,0:T(8,128)(2,1)} async-done(((bf16[768,3072]{1,0:T(8,128)(2,1)}), bf16[48,3072]{1,0:T(8,128)(2,1)}) %reduce-scatter.18.cloned.1.call-update) | async-done | bytes 294928 | tf_op jit(solution)/shard_map/reduce_scatter | solution.py:259
  520.3 79.0 %reduce-scatter.20.cloned.1.call-done = bf16[48,3072]{1,0:T(8,128)(2,1)} async-done(((bf16[768,3072]{1,0:T(8,128)(2,1)}), bf16[48,3072]{1,0:T(8,128)(2,1)}) %reduce-scatter.20.cloned.1.call-update) | async-done | bytes 294928 | tf_op jit(solution)/shard_map/reduce_scatter | solution.py:262
  599.3 70.8 %reduce-scatter.14.cloned.1.call-done = bf16[48,2304]{1,0:T(8,128)(2,1)} async-done(((bf16[768,2304]{1,0:T(8,128)(2,1)}), bf16[48,2304]{1,0:T(8,128)(2,1)}) %reduce-scatter.14.cloned.1.call-update) | async-done | bytes 221200 | tf_op jit(solution)/shard_map/reduce_scatter | solution.py:253
  670.2 2.1 pad_maximum_fusion.1
  673.2 53.5 %reduce-scatter.22.cloned.1.call-done = bf16[48,15]{1,0:T(8,128)(2,1)} async-done(((bf16[768,15]{1,0:T(8,128)(2,1)}), bf16[48,15]{1,0:T(8,128)(2,1)}) %reduce-scatter.22.cloned.1.call-update) | async-done | bytes 1456
  727.5 4.9 psum.15
  733.6 31.4 %all-reduce.2.cloned.1.call-done = bf16[48,9216]{1,0:T(8,128)(2,1)} async-done(((bf16[48,9216]{1,0:T(8,128)(2,1)}), bf16[48,9216]{1,0:T(8,128)(2,1)}) %all-reduce.2.cloned.1.call-update) | async-done | bytes 884752 | tf_op jit(solution)/shard_map/psum | solution.py:271
  765.0 5.7 multiply_add_fusion
  (143 shorter events, 15.1 us)
Async XLA Ops:
  7.2 26.7 %copy-start = (s32[1,1024]{1,0:T(1,128)S(1)}, s32[1,1024]{1,0:T(1,128)}, u32[]{:S(2)}) copy-start(s32[1,1024]{1,0:T(1,128)} %param.11) | copy-start | bytes 12292
  7.2 27.3 %copy-start.16 = (bf16[1,512,768]{2,1,0:T(8,128)(2,1)S(1)}, bf16[1,512,768]{2,1,0:T(8,128)(2,1)}, u32[]{:S(2)}) copy-start(bf16[1,512,768]{2,1,0:T(8,128)(2,1)} %param.10) | copy-start | bytes 2359300
  7.2 53.4 %all-gather.10.cloned.1.call-start = ((), (), s32[]{:S(2)}) async-start(), calls=%async_computation.7 | async-start | bytes 3760128 | tf_op jit(solution)/shard_map/all_gather | solution.py:123
  9.6 82.7 %all-gather.20.cloned.1.call-start = ((), (), s32[]{:S(2)}) async-start(), calls=%async_computation.19 | async-start | bytes 2359296 | tf_op jit(solution)/shard_map/all_gather | solution.py:149
  33.9 0.6 copy-start.22
  34.9 25.7 %copy-start.15 = (f32[512,768]{1,0:T(8,128)}, f32[512,768]{1,0:T(8,128)S(1)}, u32[]{:S(2)}) copy-start(f32[512,768]{1,0:T(8,128)S(1)} %convert_add_fusion) | copy-start | bytes 4718596
  64.6 4.6 copy-start.27
  65.9 55.7 %all-gather.18.cloned.1.call-start = ((), (), s32[]{:S(2)}) async-start(), calls=%async_computation.18 | async-start | bytes 2359296 | tf_op jit(solution)/shard_map/all_gather | solution.py:150
  66.7 96.1 %all-gather.12.cloned.1.call-start = ((), (), s32[]{:S(2)}) async-start(), calls=%async_computation.8 | async-start | bytes 1253376 | tf_op jit(solution)/shard_map/all_gather | solution.py:124
  67.4 150.4 %all-gather.14.cloned.1.call-start = ((), (), s32[]{:S(2)}) async-start(), calls=%async_computation.9 | async-start | bytes 5013504 | tf_op jit(solution)/shard_map/all_gather | solution.py:125
  68.3 204.2 %all-gather.16.cloned.1.call-start = ((), (), s32[]{:S(2)}) async-start(), calls=%async_computation.10 | async-start | bytes 5013504 | tf_op jit(solution)/shard_map/all_gather | solution.py:128
  68.9 314.1 %reduce-scatter.12.cloned.1.call-start = ((), (), s32[]{:S(2)}) async-start(), calls=%async_computation.12 | async-start | bytes 2359296 | tf_op jit(solution)/shard_map/reduce_scatter | solution.py:208
  69.6 35.1 %copy-start.5 = (bf16[512,768]{0,1:T(8,128)(2,1)}, bf16[512,768]{0,1:T(8,128)(2,1)S(1)}, u32[]{:S(2)}) copy-start(bf16[512,768]{0,1:T(8,128)(2,1)S(1)} %copy.36) | copy-start | bytes 2359300
  94.0 10.7 %copy-start.3 = (bf16[1024,768]{0,1:T(8,128)(2,1)}, bf16[1024,768]{0,1:T(8,128)(2,1)S(1)}, u32[]{:S(2)}) copy-start(bf16[1024,768]{0,1:T(8,128)(2,1)S(1)} %copy.37) | copy-start | bytes 4718596
  165.7 72.3 %copy-start.11 = (f32[512,768]{1,0:T(8,128)}, f32[512,768]{1,0:T(8,128)S(1)}, u32[]{:S(2)}) copy-start(f32[512,768]{1,0:T(8,128)S(1)} %get-tuple-element.106) | copy-start | bytes 4718596
  272.5 6.9 copy-start.8
  279.1 2.9 copy-start.31
  279.4 4.5 copy-start.28
  280.2 10.8 %slice-start = ((s8[4718592]{0:T(1024)(128)(4,1)}), s8[4194304]{0:T(1024)(128)(4,1)S(1)}, s32[]{:S(2)}) async-start(s8[4718592]{0:T(1024)(128)(4,1)} %bitcast.93), calls=%async_computation.21 | async-start | bytes 8388608
  282.0 8.9 %copy-start.17 = (bf16[512,768]{1,0:T(8,128)(2,1)}, bf16[512,768]{1,0:T(8,128)(2,1)S(1)}, u32[]{:S(2)}) copy-start(bf16[512,768]{1,0:T(8,128)(2,1)S(1)} %get-tuple-element.82) | copy-start | bytes 2359300
  283.9 7.1 copy-start.12
  283.9 7.1 slice-start.1
  290.9 3.2 copy-start.30
  294.2 2.9 copy-start.29
  294.8 1.1 copy-start.9
  296.2 0.9 copy-start.19
  312.6 70.3 %reduce-scatter.10.cloned.1.call-start = ((), (), s32[]{:S(2)}) async-start(), calls=%async_computation.11 | async-start | bytes 2359296 | tf_op jit(solution)/shard_map/reduce_scatter | solution.py:205
  333.5 16.9 %copy-start.6 = (bf16[512,768]{0,1:T(8,128)(2,1)S(1)}, bf16[512,768]{0,1:T(8,128)(2,1)}, u32[]{:S(2)}) copy-start(bf16[512,768]{0,1:T(8,128)(2,1)} %copy-done.5) | copy-start | bytes 2359300
  350.4 5.1 copy-start.2
  350.4 5.2 copy-start.20
  355.5 3.2 copy-start.13
  355.5 86.5 %reduce-scatter.16.cloned.1.call-start = ((), (), s32[]{:S(2)}) async-start(), calls=%async_computation.14 | async-start | bytes 1253376 | tf_op jit(solution)/shard_map/reduce_scatter | solution.py:256
  358.6 161.7 %reduce-scatter.18.cloned.1.call-start = ((), (), s32[]{:S(2)}) async-start(), calls=%async_computation.15 | async-start | bytes 5013504 | tf_op jit(solution)/shard_map/reduce_scatter | solution.py:259
  365.5 1.1 copy-start.18
  365.5 233.8 %reduce-scatter.20.cloned.1.call-start = ((), (), s32[]{:S(2)}) async-start(), calls=%async_computation.16 | async-start | bytes 5013504 | tf_op jit(solution)/shard_map/reduce_scatter | solution.py:262
  372.9 1.4 copy-start.4
  372.9 297.2 %reduce-scatter.14.cloned.1.call-start = ((), (), s32[]{:S(2)}) async-start(), calls=%async_computation.13 | async-start | bytes 3760128 | tf_op jit(solution)/shard_map/reduce_scatter | solution.py:253
  382.9 6.3 copy-start.14
  388.9 2.3 copy-start.10
  388.9 337.8 %reduce-scatter.22.cloned.1.call-start = ((), (), s32[]{:S(2)}) async-start(), calls=%async_computation.20 | async-start | bytes 208896
  391.2 5.0 copy-start.23
  396.1 336.3 %copy-start.21 = (f32[48,15]{0,1:T(8,128)S(1)}, f32[48,15]{0,1:T(8,128)}, u32[]{:S(2)}) copy-start(f32[48,15]{0,1:T(8,128)} %param.17) | copy-start | bytes 8644
  396.2 336.3 %copy-start.24 = (f32[48,15]{0,1:T(8,128)S(1)}, f32[48,15]{0,1:T(8,128)}, u32[]{:S(2)}) copy-start(f32[48,15]{0,1:T(8,128)} %param.19) | copy-start | bytes 8644
  396.2 336.3 %copy-start.25 = (f32[48,15]{0,1:T(8,128)S(1)}, f32[48,15]{0,1:T(8,128)}, u32[]{:S(2)}) copy-start(f32[48,15]{0,1:T(8,128)} %param.18) | copy-start | bytes 8644
  396.2 368.8 %copy-start.7 = (f32[48,9216]{1,0:T(8,128)S(1)}, f32[48,9216]{1,0:T(8,128)}, u32[]{:S(2)}) copy-start(f32[48,9216]{1,0:T(8,128)} %param.14) | copy-start | bytes 5308420
  397.9 367.1 %all-reduce.2.cloned.1.call-start = ((), (), s32[]{:S(2)}) async-start(), calls=%async_computation.17 | async-start | bytes 1769472 | tf_op jit(solution)/shard_map/psum | solution.py:271
  733.1 37.7 %copy-start.26 = (f32[48,15]{0,1:T(8,128)}, f32[48,15]{0,1:T(8,128)S(1)}, u32[]{:S(2)}) copy-start(f32[48,15]{0,1:T(8,128)S(1)} %get-tuple-element.78) | copy-start | bytes 8644
  733.1 37.7 %copy-start.1 = (s32[1,1024]{1,0:T(1,128)S(1)}, s32[1,1024]{1,0:T(1,128)}, u32[]{:S(2)}) copy-start(s32[1,1024]{1,0:T(1,128)} %param.11) | copy-start | bytes 12292
Sparse Core Ops, SparseCore 0:
  10.9 49.6 all-gather.9
  66.0 26.1 all-gather.19
  94.4 27.2 all-gather.17
  124.4 38.3 all-gather.11
  165.4 52.3 all-gather.13
  220.5 51.9 all-gather.15
  312.8 24.5 reduce-scatter.11
  355.6 24.6 reduce-scatter.9
  383.9 58.0 reduce-scatter.15
  445.7 74.5 reduce-scatter.17
  524.7 74.5 reduce-scatter.19
  603.0 67.0 reduce-scatter.13
  674.2 52.4 reduce-scatter.21
  729.5 35.4 all-reduce.1
where the time goes:
time: 781 us; the launch traced here: 778 us
  waiting for transfers between devices  526 us (67%)
  matrix products  142 us (18%)
  other arithmetic  46.1 us (6%)
  blocking collectives  28.3 us (4%)
  local copies, waits for them, and re-layouts  18.8 us (2%)
  between operations  14.8 us (2%)
    reduce_scatter x1, waiting for transfers between devices, per_device(): lax.psum_scatter(grad_w_down.astype(jnp.bfloat16), 'dp', scatter_dimensio...  79 us
    reduce_scatter x1, waiting for transfers between devices, per_device(): lax.psum_scatter(grad_w_up.astype(jnp.bfloat16), 'dp', scatter_dimension=...  78.3 us
    reduce_scatter x1, waiting for transfers between devices, per_device(): lax.psum_scatter(grad_w_qkv.astype(jnp.bfloat16), 'dp', scatter_dimension...  70.8 us
    unnamed x15, waiting for transfers between devices  54.9 us
    all_gather x1, waiting for transfers between devices, per_device(): lax.all_gather(low_mats[:, 4 * MODEL_WIDTH:4 * MODEL_WIDTH + FF], 'dp', a...  51.8 us
    reduce_scatter x1, waiting for transfers between devices, per_device(): lax.psum_scatter(grad_w_out.astype(jnp.bfloat16), 'dp', scatter_dimension...  44.1 us
    all_gather x1, waiting for transfers between devices, per_device(): lax.all_gather(low_mats[:, 4 * MODEL_WIDTH + FF:], 'dp', axis=0, tiled=True)  34.6 us
    dot_general x5, matrix products, product(): return jnp.dot(left, right, preferred_element_type=jnp.float32)  34.5 us
  transfers between devices with their start and end apart: 14, of which 12 were waited for; matrix products, arithmetic and copies ran while one was open for 19% of the time, Pallas kernels for 0%

commit v1 on v0

--- a/solution.py
+++ b/solution.py
@@ -1,8 +1,11 @@
+import functools
 import math
 
 import jax
 import jax.numpy as jnp
 from jax import lax
+from jax.experimental import pallas as pl
+from jax.experimental.pallas import tpu as pltpu
 from jax.sharding import PartitionSpec as P
 
 MODEL_WIDTH = 768
@@ -296,6 +299,462 @@
     )
 
 
+LN2 = math.log(2.0)
+NT = (((1,), (1,)), ((), ()))
+NN = (((1,), (0,)), ((), ()))
+
+
+def mxu(left, right, dims):
+    return lax.dot_general(left, right, dims, preferred_element_type=jnp.float32)
+
+
+def three_parts(value):
+    high = value.astype(jnp.bfloat16)
+    rest = value - high.astype(jnp.float32)
+    middle = rest.astype(jnp.bfloat16)
+    return high, middle, (rest - middle.astype(jnp.float32)).astype(jnp.bfloat16)
+
+
+def attend_kernel(q_ref, k_ref, v_ref, masked_ref, out_ref, log_ref, *, block):
+    length = k_ref.shape[0]
+    lane = lax.broadcasted_iota(jnp.int32, (1, 128), 1)
+    keys = jnp.concatenate([k_ref[...], masked_ref[...]], axis=1)
+    values = jnp.concatenate([v_ref[...], jnp.ones((length, 128), jnp.bfloat16)], axis=1)
+    one = jnp.broadcast_to(jnp.where(lane == 0, 1.0, 0.0).astype(jnp.bfloat16), (block, 128))
+    for i in range(q_ref.shape[0] // block):
+        span = slice(i * block, (i + 1) * block)
+        query = q_ref[span, :]
+        outs, logs = [], []
+        for head in range(2):
+            here = (lane < 64) if head == 0 else (lane >= 64)
+            only = jnp.where(here, query, jnp.zeros_like(query))
+            scores = mxu(jnp.concatenate([only, one], axis=1), keys, NT)
+            top = jnp.max(scores, axis=1, keepdims=True)
+            weight = jnp.exp2(scores - top).astype(jnp.bfloat16)
+            mixed = mxu(weight, values, NN)
+            total = mixed[:, 128:]
+            outs.append(mixed[:, :128] / total)
+            logs.append(top + jnp.log2(total[:, 0:1]))
+        out_ref[span, :] = jnp.where(lane < 64, outs[0], outs[1]).astype(jnp.bfloat16)
+        log_ref[span, :] = jnp.where(lane == 0, logs[0], jnp.where(lane == 1, logs[1], 0.0))
+
+
+def attend(qkv, masked, block=256):
+    length, columns = qkv.shape
+    pairs = columns // 3 // 128
+
+    def spec(first):
+        return pl.BlockSpec((length, 128), lambda i: (0, first + i))
+
+    return pl.pallas_call(
+        functools.partial(attend_kernel, block=block),
+        grid=(pairs,),
+        in_specs=[
+            spec(0),
+            spec(pairs),
+            spec(2 * pairs),
+            pl.BlockSpec((length, 128), lambda i: (0, 0)),
+        ],
+        out_specs=[spec(0), spec(0)],
+        out_shape=[
+            jax.ShapeDtypeStruct((length, pairs * 128), jnp.bfloat16),
+            jax.ShapeDtypeStruct((length, pairs * 128), jnp.float32),
+        ],
+        compiler_params=pltpu.CompilerParams(vmem_limit_bytes=24 * 2**20),
+        cost_estimate=pl.CostEstimate(
+            flops=length * length * pairs * 2 * 128 * 8,
+            bytes_accessed=length * columns * 4,
+            transcendentals=length * length * pairs * 2,
+        ),
+        name="attend",
+    )(qkv, qkv, qkv, masked)
+
+
+def attend_back_kernel(
+    q_ref, k_ref, v_ref, o_ref, g_ref, log_ref, masked_ref, dq_ref, dk_ref, dv_ref, dk_sum, dv_sum, *, block
+):
+    length = k_ref.shape[0]
+    bf16 = jnp.bfloat16
+    lane = lax.broadcasted_iota(jnp.int32, (1, 128), 1)
+    ones = jnp.where((lane >= 1) & (lane <= 3), 1.0, 0.0).astype(bf16)
+    masked = masked_ref[...]
+    keys = jnp.concatenate(
+        [k_ref[...], jnp.where(lane == 0, masked, jnp.broadcast_to(ones, masked.shape))], axis=1
+    )
+    three = jnp.broadcast_to(jnp.where(lane <= 2, 1.0, 0.0).astype(bf16), (length, 128))
+    values = jnp.concatenate([v_ref[...], three], axis=1)
+    keys_t = k_ref[...].T
+    one = jnp.ones((block, 128), bf16)
+    zero = jnp.zeros((block, 128), bf16)
+    row = lax.broadcasted_iota(jnp.int32, (128, 1), 0)
+    for i in range(q_ref.shape[0] // block):
+        span = slice(i * block, (i + 1) * block)
+        query, grad = q_ref[span, :], g_ref[span, :]
+        both = grad.astype(jnp.float32) * o_ref[span, :].astype(jnp.float32)
+        logs = log_ref[span, :]
+        turned = []
+        for head in range(2):
+            here = (lane < 64) if head == 0 else (lane >= 64)
+            inner = jnp.sum(jnp.where(here, both, 0.0), axis=1, keepdims=True)
+            wide = lambda t: jnp.broadcast_to(t, (block, 128))
+            i0, i1, i2 = (wide(t) for t in three_parts(-inner))
+            l0, l1, l2 = (wide(t) for t in three_parts(-logs[:, head : head + 1]))
+            query_h = jnp.where(here, query, zero)
+            grad_h = jnp.where(here, grad, zero)
+            tail_q = jnp.where(
+                lane == 0,
+                one,
+                jnp.where(lane == 1, l0, jnp.where(lane == 2, l1, jnp.where(lane == 3, l2, zero))),
+            )
+            tail_g = jnp.where(lane == 0, i0, jnp.where(lane == 1, i1, jnp.where(lane == 2, i2, zero)))
+            prob = jnp.exp2(mxu(keys, jnp.concatenate([query_h, tail_q], axis=1), NT))
+            slope = mxu(values, jnp.concatenate([grad_h, tail_g], axis=1), NT)
+            grad_scores = (prob * slope).astype(bf16)
+            add_v = mxu(prob.astype(bf16), grad_h, NN)
+            add_k = mxu(grad_scores, query_h, NN)
+            if i == 0 and head == 0:
+                dv_sum[...] = add_v
+                dk_sum[...] = add_k
+            else:
+                dv_sum[...] += add_v
+                dk_sum[...] += add_k
+            turned.append(mxu(keys_t, grad_scores, NN))
+        dq_ref[span, :] = (jnp.where(row < 64, turned[0], turned[1]) * 0.125).T.astype(bf16)
+    dk_ref[...] = (dk_sum[...] * LN2).astype(bf16)
+    dv_ref[...] = dv_sum[...].astype(bf16)
+
+
+def attend_back(qkv, out, grad, log_sum, masked, block=512):
+    length, columns = qkv.shape
+    pairs = columns // 3 // 128
+
+    def spec(first):
+        return pl.BlockSpec((length, 128), lambda i: (0, first + i))
+
+    return pl.pallas_call(
+        functools.partial(attend_back_kernel, block=block),
+        grid=(pairs,),
+        in_specs=[
+            spec(0),
+            spec(pairs),
+            spec(2 * pairs),
+            spec(0),
+            spec(0),
+            spec(0),
+            pl.BlockSpec((length, 128), lambda i: (0, 0)),
+        ],
+        out_specs=[spec(0)] * 3,
+        out_shape=[jax.ShapeDtypeStruct((length, pairs * 128), jnp.bfloat16)] * 3,
+        scratch_shapes=[pltpu.VMEM((length, 128), jnp.float32)] * 2,
+        compiler_params=pltpu.CompilerParams(vmem_limit_bytes=32 * 2**20),
+        cost_estimate=pl.CostEstimate(
+            flops=length * length * pairs * 2 * 128 * 20,
+            bytes_accessed=length * columns * 8,
+            transcendentals=length * length * pairs * 2,
+        ),
+        name="attend_back",
+    )(qkv, qkv, qkv, out, grad, log_sum, masked)
+
+
+SEQ_SWAP = [(0, 1), (1, 0)]
+CORE_SWAP = [(i, i ^ 1) for i in range(16)]
+Y_SWAP = [(i, i ^ 2) for i in range(16)]
+Z_LINES = [[r + 4 * z for z in range(4)] for r in range(4)]
+HALF = MODEL_WIDTH // 2
+FHALF = FF // 2
+QCOLS = 5 * 128
+BF16 = jnp.bfloat16
+F32 = jnp.float32
+
+
+def over_seq(value):
+    return lax.ppermute(value, "seq", SEQ_SWAP)
+
+
+def over_core(value):
+    return lax.ppermute(value, "dp", CORE_SWAP)
+
+
+def over_y(value):
+    return lax.ppermute(value, "dp", Y_SWAP)
+
+
+def over_z(blocks):
+    return lax.all_to_all(blocks, "dp", 0, 0, axis_index_groups=Z_LINES)
+
+
+def ordered(flag, mine, theirs, axis):
+    return jnp.where(
+        flag == 0,
+        jnp.concatenate([mine, theirs], axis=axis),
+        jnp.concatenate([theirs, mine], axis=axis),
+    )
+
+
+def part(value, index, size, axis):
+    return lax.dynamic_slice_in_dim(value, index * size, size, axis)
+
+
+def gelu_and_slope(up):
+    size = jnp.abs(up)
+    t = 1.0 / (1.0 + (0.3275911 * math.sqrt(0.5)) * size)
+    bell = jnp.exp(-0.5 * up * up)
+    poly = t * (
+        0.5 * 0.254829592
+        + t
+        * (
+            0.5 * -0.284496736
+            + t * (0.5 * 1.421413741 + t * (0.5 * -1.453152027 + t * (0.5 * 1.061405429)))
+        )
+    )
+    tail = poly * bell
+    below = jnp.where(up < 0, tail, 1.0 - tail)
+    return up * below, below + up * bell * (1.0 / math.sqrt(2.0 * math.pi))
+
+
+def norm_parts(rows):
+    mean = jnp.mean(rows, axis=-1, keepdims=True)
+    centred = rows - mean
+    spread = jnp.mean(centred * centred, axis=-1, keepdims=True)
+    scale = lax.rsqrt(spread + epsilon)
+    return centred * scale, scale
+
+
+def norm_back(grad, unit, scale, gain):
+    grad_gain = jnp.sum(unit * grad, axis=0)
+    grad_shift = jnp.sum(grad, axis=0)
+    inner = grad * gain
+    mean_one = jnp.mean(inner, axis=-1, keepdims=True)
+    mean_two = jnp.mean(inner * unit, axis=-1, keepdims=True)
+    return scale * (inner - mean_one - unit * mean_two), grad_gain, grad_shift
+
+
+def reduce_rows(grad, y):
+    n = grad.shape[1]
+    grouped = grad.reshape(4, 2, 96, n)
+    mine = lax.dynamic_index_in_dim(grouped, y, 1, keepdims=False)
+    theirs = lax.dynamic_index_in_dim(grouped, 1 - y, 1, keepdims=False)
+    got = over_y(theirs)
+    summed = (mine.astype(F32) + got.astype(F32)).astype(BF16)
+    lines = over_z(summed)
+    return jnp.sum(lines.astype(F32), axis=0)
+
+
+def tuned(
+    inputs,
+    modality,
+    key_valid_mask,
+    output_gradient,
+    mats,
+    mats_momentum,
+    mats_average,
+    smalls,
+    smalls_momentum,
+    smalls_average,
+):
+    width = MODEL_WIDTH
+    rows = inputs.shape[1]
+    dp = lax.axis_index("dp")
+    x = lax.axis_index("seq")
+    core = dp % 2
+    y = (dp // 2) % 2
+    low = mats.astype(BF16)
+
+    attention_block = jnp.concatenate(
+        [part(low[:, j * width : (j + 1) * width], x, HALF, 1) for j in range(3)]
+        + [low[:, 3 * width : 4 * width], jnp.pad(smalls.astype(BF16), ((0, 0), (0, 113)))],
+        axis=1,
+    )
+    shared = low[:, 4 * width :].reshape(48, 2, 2, FHALF)
+    keep = lax.dynamic_index_in_dim(shared, core, 2, keepdims=False)
+    give = lax.dynamic_index_in_dim(shared, 1 - core, 2, keepdims=False)
+    other_inputs = over_seq(inputs[0])
+    att_z = over_z(jnp.broadcast_to(attention_block[None], (4,) + attention_block.shape))
+    took = over_core(give)
+    pair = ordered(core, keep[None], took[None], 0)
+    up_block = pair[:, :, 0].reshape(96, FHALF)
+    down_block = pair[:, :, 1].reshape(96, FHALF)
+    att_y = ordered(y, att_z[:, None], over_y(att_z)[:, None], 1)
+    att_w = ordered(core, att_y[:, :, None], over_core(att_y)[:, :, None], 2).reshape(width, -1)
+    up_z = over_z(jnp.broadcast_to(up_block[None], (4, 96, FHALF)))
+    down_z = over_z(jnp.broadcast_to(down_block[None], (4, 96, FHALF)))
+    w_up = ordered(y, up_z[:, None], over_y(up_z)[:, None], 1).reshape(width, FHALF)
+    w_down = ordered(y, down_z[:, None], over_y(down_z)[:, None], 1).reshape(width, FHALF)
+    w_qkv = att_w[:, 0 : 3 * HALF]
+    w_out = att_w[:, 3 * HALF : 3 * HALF + width]
+    whole_smalls = att_w[:, 3 * HALF + width : 3 * HALF + width + 15]
+    params = whole_smalls.astype(F32).T
+    bias_up = part(params[8:12].reshape(FF), core, FHALF, 0)
+    embed = whole_smalls[:, 12:15].T
+
+    leading_key = (jnp.arange(2 * rows) == 0).astype(jnp.int32)
+    live = jnp.maximum(key_valid_mask[0], leading_key)
+    own_first = lambda v: jnp.concatenate([part(v, x, rows, 0), part(v, 1 - x, rows, 0)])
+    live = own_first(live)
+    kinds = own_first(modality[0])
+    onehot = (kinds[:, None] == jnp.arange(3, dtype=jnp.int32)[None, :]).astype(BF16)
+    both_inputs = jnp.concatenate([inputs[0], other_inputs], axis=0)
+    x_all = both_inputs.astype(F32) + product(onehot, embed)
+    x_low = x_all.astype(BF16)
+    x_in = x_all[0:rows]
+    bias_q = part(params[0], x, HALF, 0)
+    bias_v = part(params[1], x, HALF, 0)
+    bias_qkv = jnp.concatenate([bias_q, jnp.zeros_like(bias_q), bias_v])
+    q_scale = jnp.where(jnp.arange(3 * HALF) < HALF, 0.125 / LN2, 1.0)
+    qkv = ((product(x_low, w_qkv) + bias_qkv) * q_scale).astype(BF16)
+    masked = jnp.where(
+        (live == 0)[:, None] & (jnp.arange(128) == 0)[None, :], masked_score, 0.0
+    ).astype(BF16)
+    out_heads, log_sum = attend(qkv, masked)
+    got_heads = over_seq(out_heads[rows:])
+    out_low = ordered(x, out_heads[0:rows], got_heads, 1)
+    first_in = x_in + (product(out_low, w_out) + params[2])
+    unit1, scale1 = norm_parts(first_in)
+    first = unit1 * params[4] + params[5]
+    first_low = first.astype(BF16)
+
+    first_both = jnp.concatenate([first_low, over_core(first_low)], axis=0)
+    up = product(first_both, w_up) + bias_up
+    act, slope = gelu_and_slope(up)
+    act_low = act.astype(BF16)
+    slope = slope.astype(BF16)
+    ffo_other = product_nt(act_low[rows:], w_down).astype(BF16)
+    ffo_got = over_core(ffo_other)
+    ffo_own = product_nt(act_low[0:rows], w_down)
+    second_in = first + (ffo_own + ffo_got.astype(F32) + params[3])
+    unit2, scale2 = norm_parts(second_in)
+    block_out = (unit2 * params[6] + params[7]).astype(BF16)[None]
+
+    grad_rows = output_gradient[0].astype(F32)
+    grad_second, grad_gain2, grad_shift2 = norm_back(grad_rows, unit2, scale2, params[6])
+    grad_ffo = grad_second.astype(BF16)
+    grad_bias_down = jnp.sum(grad_ffo.astype(F32), axis=0)
+    ffo_both = jnp.concatenate([grad_ffo, over_core(grad_ffo)], axis=0)
+    grad_act = product(ffo_both, w_down)
+    grad_up_f = grad_act * slope.astype(F32)
+    grad_up = grad_up_f.astype(BF16)
+    grad_bias_up = jnp.sum(grad_up.astype(F32), axis=0)
+    grad_w_down = product_tn(ffo_both, act_low).astype(BF16)
+    down_rows = reduce_rows(grad_w_down, y)
+    back_other = over_core(product_nt(grad_up[rows:], w_up).astype(BF16))
+    back_own = product_nt(grad_up[0:rows], w_up)
+    grad_first = grad_second + back_own + back_other.astype(F32)
+    grad_w_up = product_tn(first_both, grad_up).astype(BF16)
+    grad_first_in, grad_gain1, grad_shift1 = norm_back(grad_first, unit1, scale1, params[4])
+    grad_mixed = grad_first_in.astype(BF16)
+    grad_bias_out = jnp.sum(grad_mixed.astype(F32), axis=0)
+    grad_out = product_nt(grad_mixed, w_out).astype(BF16)
+    got_grad = over_seq(part(grad_out, 1 - x, HALF, 1))
+    grad_heads = jnp.concatenate([part(grad_out, x, HALF, 1), got_grad], axis=0)
+    out_both = jnp.concatenate([out_low, over_core(out_low)], axis=0)
+    mixed_half = jnp.concatenate(
+        [part(grad_mixed, core, HALF, 1), over_core(part(grad_mixed, 1 - core, HALF, 1))], axis=0
+    )
+    grad_w_out = product_tn(out_both, mixed_half).astype(BF16)
+    up_rows = reduce_rows(jnp.concatenate([grad_w_up, grad_w_out], axis=1), y)
+
+    gq, gk, gv = attend_back(qkv, out_heads, grad_heads, log_sum, masked)
+    grad_qkv = jnp.concatenate([gq, gk, gv], axis=1)
+    x_both = jnp.concatenate([x_low, over_core(x_low)], axis=0)
+    padded = jnp.pad(grad_qkv, ((0, 0), (0, 128)))
+    qkv_half = jnp.concatenate(
+        [part(padded, core, QCOLS, 1), over_core(part(padded, 1 - core, QCOLS, 1))], axis=0
+    )
+    grad_w_qkv = product_tn(x_both, qkv_half)
+    grad_x = product_nt(grad_qkv, w_qkv)
+    got_x = over_seq(grad_x[rows:].astype(BF16))
+    grad_x_in = grad_first_in + grad_x[0:rows] + got_x.astype(F32)
+    input_grad = grad_x_in.astype(BF16)[None]
+
+    hot = onehot.astype(F32)
+    high = dict(precision=lax.Precision.HIGHEST, preferred_element_type=F32)
+    rows_t = (((0,), (0,)), ((), ()))
+    grad_embed = lax.dot_general(hot, grad_x, rows_t, **high) + lax.dot_general(
+        hot[0:rows], grad_first_in, rows_t, **high
+    )
+    spread = lambda v: lax.dynamic_update_slice(jnp.zeros((width,), F32), v, (x * HALF,))
+    bias_up_all = lax.dynamic_update_slice(jnp.zeros((FF,), F32), grad_bias_up, (core * FHALF,))
+    small_rows = jnp.concatenate(
+        [
+            jnp.stack(
+                [
+                    spread(jnp.sum(gq.astype(F32), axis=0)),
+                    spread(jnp.sum(gv.astype(F32), axis=0)),
+                    grad_bias_out,
+                    grad_bias_down,
+                    grad_gain1,
+                    grad_shift1,
+                    grad_gain2,
+                    grad_shift2,
+                ]
+            ),
+            bias_up_all.reshape(4, width),
+            grad_embed,
+            jnp.zeros((1, width), F32),
+        ],
+        axis=0,
+    )
+    small_chip = small_rows + over_core(small_rows)
+    small_tile = jnp.pad(small_chip.T, ((0, 0), (0, 112)))
+    last = jnp.where(core == 0, grad_w_qkv[:, 4 * 128 :], small_tile)
+    q_rows = reduce_rows(
+        jnp.concatenate([grad_w_qkv[:, 0 : 4 * 128], last], axis=1).astype(BF16), y
+    )
+
+    def finish(value):
+        mine = part(value, core, 48, 0)
+        theirs = part(value, 1 - core, 48, 0)
+        return ordered(core, mine[:, None], over_core(theirs)[:, None], 1)
+
+    def add_seq(value):
+        sent = value.astype(BF16)
+        return (value + over_seq(sent).astype(F32)).astype(BF16)
+
+    down_own = finish(add_seq(down_rows)).reshape(48, FF)
+    up_own = finish(add_seq(up_rows))
+    q_low = q_rows.astype(BF16)
+    q_pair = jnp.concatenate([q_low, over_seq(q_low)], axis=1)
+    q_own = finish(q_pair).reshape(48, 2, 2, QCOLS)
+    mine_q = q_own[:, :, 0].reshape(48, 2 * QCOLS)
+    other_q = q_own[:, :, 1].reshape(48, 2 * QCOLS)
+    pieces = [
+        ordered(x, mine_q[:, j * HALF : (j + 1) * HALF], other_q[:, j * HALF : (j + 1) * HALF], 1)
+        for j in range(3)
+    ]
+    mats_grad = jnp.concatenate(
+        pieces
+        + [up_own[:, :, FHALF:].reshape(48, width), up_own[:, :, 0:FHALF].reshape(48, FF), down_own],
+        axis=1,
+    ).astype(F32)
+    smalls_grad = mine_q[:, 3 * HALF : 3 * HALF + 15].astype(F32) + other_q[
+        :, 3 * HALF : 3 * HALF + 15
+    ].astype(F32)
+
+    out_bias_grad = smalls_grad[:, 2]
+    total_tokens = rows * lax.axis_size("dp") * lax.axis_size("seq")
+    rate = base_rate / math.sqrt(total_tokens)
+    decayed = mats_grad + decay_rate * mats
+    new_mats_momentum = momentum_rate * mats_momentum + decayed
+    new_mats = mats - rate * (decayed + momentum_rate * new_mats_momentum)
+    new_mats_average = average_rate * mats_average + (1.0 - average_rate) * new_mats
+    new_smalls_momentum = momentum_rate * smalls_momentum + smalls_grad
+    new_smalls = smalls - rate * (smalls_grad + momentum_rate * new_smalls_momentum)
+    new_smalls_average = average_rate * smalls_average + (1.0 - average_rate) * new_smalls
+    return (
+        block_out,
+        input_grad,
+        mats_grad,
+        new_mats,
+        new_mats_momentum,
+        new_mats_average,
+        smalls_grad,
+        out_bias_grad,
+        new_smalls,
+        new_smalls_momentum,
+        new_smalls_average,
+    )
+
+
 def solution(mesh):
     placed = (
         P("dp", "seq", None),
@@ -309,8 +768,9 @@
         P("dp", None),
         P("dp", None),
     )
+    plan = tuned if tuple(mesh.shape.values()) == (16, 2) else per_device
     return jax.shard_map(
-        per_device,
+        plan,
         mesh=mesh,
         in_specs=placed,
         out_specs=(

time: 781 us -> 406 us (0.52)
  waiting for transfers between devices: 526 us -> 146 us
  matrix products: 142 us -> 62.2 us
  starting transfers between devices: 1.08 us -> 41.2 us
  Pallas kernels: 0 us -> 27.6 us
  local copies, waits for them, and re-layouts: 18.8 us -> 44.6 us
  between operations: 14.8 us -> 2.5 us
    reduce_scatter x6 -> x0, waiting for transfers between devices: 272 us -> none  [the longest x1 79 us: per_device(): lax.psum_scatter(grad_w_down.astype(jnp.bfloat16), 'dp', scatter_dimensio...]
    all_gather x6 -> x0, waiting for transfers between devices: 168 us -> none  [the longest x1 51.8 us: per_device(): lax.all_gather(low_mats[:, 4 * MODEL_WIDTH:4 * MODEL_WIDTH + FF], 'dp', a...]
    ppermute x0 -> x27, waiting for transfers between devices: none -> 88 us  [the longest x6 74.3 us: over_y(): return lax.ppermute(value, 'dp', Y_SWAP)]
    dot_general x7 -> x2, matrix products: 69.3 us -> 1.95 us  [the longest x1 1.31 us: tuned(): lax.dot_general(hot, grad_x, rows_t, **high)]
    all_to_all x0 -> x5, waiting for transfers between devices: none -> 58.5 us  [over_z(): return lax.all_to_all(blocks, 'dp', 0, 0, axis_index_groups=Z_LINES)]
    unnamed x15 -> x0, waiting for transfers between devices: 54.9 us -> none
    psum x1 -> x0, waiting for transfers between devices: 31.4 us -> none  [per_device(): lax.psum(mats_shard.astype(jnp.bfloat16), 'seq').astype(jnp.float32)]
    pallas_call x0 -> x2, Pallas kernels: none -> 27.6 us  [the longest x1 18 us: attend_back(): pl.pallas_call(functools.partial(attend_back_kernel, block=block), grid=(...]
  transfers between devices with their start and end apart: 14 -> 32, of which waited for: 12 -> 13; matrix products, arithmetic and copies ran while one was open for 19% -> 30% of each run, Pallas kernels for 0% -> 7%
where the time goes in v1:
time: 406 us; the launch traced here: 400 us
  waiting for transfers between devices  146 us (36%)
  matrix products  62.2 us (15%)
  other arithmetic  49.1 us (12%)
  local copies, waits for them, and re-layouts  44.6 us (11%)
  starting transfers between devices  41.2 us (10%)
  Pallas kernels  27.6 us (7%)
  blocking collectives  26.2 us (6%)
    ppermute x6, waiting for transfers between devices, over_y(): return lax.ppermute(value, 'dp', Y_SWAP)  74.3 us
    all_to_all x5, waiting for transfers between devices, over_z(): return lax.all_to_all(blocks, 'dp', 0, 0, axis_index_groups=Z_LINES)  58.5 us
    dot_general x5, matrix products, product(): return jnp.dot(left, right, preferred_element_type=jnp.float32)  31.4 us
    all_to_all x1, blocking collectives, over_z(): return lax.all_to_all(blocks, 'dp', 0, 0, axis_index_groups=Z_LINES)  26.2 us
    all_to_all x5, starting transfers between devices, over_z(): return lax.all_to_all(blocks, 'dp', 0, 0, axis_index_groups=Z_LINES)  21.9 us
    pallas_call x1, Pallas kernels, attend_back(): pl.pallas_call(functools.partial(attend_back_kernel, block=block), grid=(...  18 us
    dot_general x4, matrix products, product_tn(): lax.dot_general(left, right, (((0,), (0,)), ((), ())), preferred_element_...  17 us
    select_n x9, other arithmetic, ordered(): jnp.where(flag == 0, jnp.concatenate([mine, theirs], axis=axis), jnp.conc...  15.1 us
  transfers between devices with their start and end apart: 32, of which 13 were waited for; matrix products, arithmetic and copies ran while one was open for 30% of the time, Pallas kernels for 7%

profile of v1, /device:TPU:0, one launch (start us, length us, event | category | flops | bytes accessed | tf_op | source)
XLA Modules:
  0.0 399.9 jit_solution(12446696743675413506)
XLA Ops:
  0.7 1.6 convert_element_type.180
  2.6 26.2 %all_to_all.30 = bf16[4,48,2048]{2,1,0:T(8,128)(2,1)S(1)} all-to-all(bf16[4,48,2048]{2,1,0:T(8,128)(2,1)S(1)} %broadcast_in_dim.106), channel_id=1, replica_groups={{0,8,16,24},{2,10,18,26},{4,12,20,28},{6,14,22,30},{1,9,17,25},{3,11,19..., dimensions={0} | all-to-all | bytes 1572864 | tf_op jit(solution)/shard_map/all_to_all | solution.py:483
  35.8 11.2 %collective-permute-done.1 = bf16[4,48,2048]{2,1,0:T(8,128)(2,1)S(1)} collective-permute-done((bf16[4,48,2048]{2,1,0:T(8,128)(2,1)S(1)}, bf16[4,48,2048]{2,1,0:T(8,128)(2,1)S(1)}, u32[]{:S(2)}, u32[]{:S(2)}) %collective-permute-start.1) | collective-permute-done | bytes 786464 | tf_op jit(solution)/shard_map/ppermute | solution.py:479
  50.0 3.5 all-to-all-start.1
  53.8 2.9 maximum_select_fusion
  59.0 4.0 %fusion.97 = (bf16[1024,768]{1,0:T(8,128)(2,1)}, f32[1024,768]{1,0:T(8,128)}) fusion(bf16[768,2048]{1,0:T(8,128)(2,1)S(1)} %bitcast.129, s32[1024]{0:T(1024)S(1)} %pad_add_fusion, bf16[512,768]{1,0:T(8,128)(2,1)} %collective-permute-done, bf16[512,768]{1,0:T(8,128)(2,1)S(1)} %bitcast.152), kind=kOutput, calls=%fused_computation.222 | convolution fusion | flops 9440256 | bytes 6492160 | tf_op jit(solution)/shard_map/dot_general | solution.py:26
  63.0 20.0 %all-to-all-done.1 = bf16[4,96,1536]{2,1,0:T(8,128)(2,1)S(1)} async-done(((bf16[4,96,1536]{2,1,0:T(8,128)(2,1)}), bf16[4,96,1536]{2,1,0:T(8,128)(2,1)S(1)}, u32[]{:S(2)}, u32[]{:S(2)}) %all-to-all-start.1) | async-done | bytes 1179680 | tf_op jit(solution)/shard_map/all_to_all | solution.py:483
  84.4 4.8 %all-to-all-start.2 = ((bf16[4,96,1536]{2,1,0:T(8,128)(2,1)}), bf16[4,96,1536]{2,1,0:T(8,128)(2,1)}, u32[]{:S(2)}, u32[]{:S(2)}) async-start(bf16[4,96,1536]{2,1,0:T(8,128)(2,1)} %broadcast_in_dim.122), calls=%async_computation.2 | async-start | bytes 2359296 | tf_op jit(solution)/shard_map/all_to_all | solution.py:483
  89.2 4.2 %multiply_convert_fusion.2.q_ref.k_ref.v_ref = bf16[1024,1152]{1,0:T(8,128)(2,1)S(1)} fusion(bf16[1024,768]{1,0:T(8,128)(2,1)} %get-tuple-element.127, f32[1152]{0:T(1024)S(1)} %fusion.81, f32[1152]{0:T(1024)S(1)} %pad_maximum_fusion.8, bf16[768,2048]{1,0:T(8,128)(2,1)} %bitcast.130), kind=kOutput, calls=%fused_computation.11 | convolution fusion | flops 1815478272 | bytes 5710848 | tf_op jit(solution)/shard_map/dot_general | solution.py:26
  93.4 9.5 %attend.1 = (bf16[1024,384]{1,0:T(8,128)(2,1)S(1)}, f32[1024,384]{1,0:T(8,128)S(1)}) custom-call(bf16[1024,1152]{1,0:T(8,128)(2,1)S(1)} %multiply_convert_fusion.2.q_ref.k_ref.v_ref, bf16[1024,1152]{1,0:T(8,128)(2,1)S(1)} %multiply_convert_fusion.2.q_ref.k_ref.v_ref, bf16[1024,1152]{1,0:T(8,128)(2,1)S(1)} %multiply_convert_fusion.2.q_ref.k_ref.v_ref, ...), custom_call_target="tpu_custom_call" | custom-call | flops 6442450944 | bytes 4718592 | tf_op jit(solution)/shard_map/attend/pallas_call | solution.py:349
  108.0 9.9 %all-to-all-done.2 = bf16[4,96,1536]{2,1,0:T(8,128)(2,1)} async-done(((bf16[4,96,1536]{2,1,0:T(8,128)(2,1)}), bf16[4,96,1536]{2,1,0:T(8,128)(2,1)}, u32[]{:S(2)}, u32[]{:S(2)}) %all-to-all-start.2) | async-done | bytes 1179680 | tf_op jit(solution)/shard_map/all_to_all | solution.py:483
  119.5 1.6 maximum_select_fusion.5
  121.1 2.9 fusion.98
  125.6 10.2 %collective-permute-done.6 = bf16[4,96,1536]{2,1,0:T(8,128)(2,1)} collective-permute-done((bf16[4,96,1536]{2,1,0:T(8,128)(2,1)}, bf16[4,96,1536]{2,1,0:T(8,128)(2,1)}, u32[]{:S(2)}, u32[]{:S(2)}) %collective-permute-start.6) | collective-permute-done | bytes 1179680 | tf_op jit(solution)/shard_map/ppermute | solution.py:479
  135.7 4.1 %maximum_select_fusion.1 = bf16[4,2,96,1536]{3,2,1,0:T(8,128)(2,1)} fusion(bf16[4,1,96,1536]{3,2,1,0:T(8,128)(2,1)} %bitcast.16, bf16[4,1,96,1536]{3,2,1,0:T(8,128)(2,1)} %bitcast.127, pred[]{:T(512)S(6)} %eq.59), kind=kLoop, calls=%fused_computation.29 | loop fusion | flops 3538944 | bytes 4718593 | tf_op jit(solution)/shard_map/jit(_where)/select_n | solution.py:487
  139.9 19.6 %collective-permute-done.7 = bf16[4,96,1536]{2,1,0:T(8,128)(2,1)} collective-permute-done((bf16[4,96,1536]{2,1,0:T(8,128)(2,1)}, bf16[4,96,1536]{2,1,0:T(8,128)(2,1)}, u32[]{:S(2)}, u32[]{:S(2)}) %collective-permute-start.7) | collective-permute-done | bytes 1179680 | tf_op jit(solution)/shard_map/ppermute | solution.py:479
  159.4 4.3 %maximum_select_fusion.2 = bf16[4,2,96,1536]{3,2,1,0:T(8,128)(2,1)} fusion(bf16[4,1,96,1536]{3,2,1,0:T(8,128)(2,1)} %bitcast.20, bf16[4,1,96,1536]{3,2,1,0:T(8,128)(2,1)} %bitcast.19, pred[]{:T(512)S(6)} %eq.59), kind=kLoop, calls=%fused_computation.30 | loop fusion | flops 3538944 | bytes 4718593 | tf_op jit(solution)/shard_map/jit(_where)/select_n | solution.py:487
  165.9 9.9 %multiply_convert_fusion.1 = (bf16[1024,1536]{1,0:T(8,128)(2,1)S(1)}, f32[1024,1536]{1,0:T(8,128)}) fusion(f32[1536]{0:T(1024)S(1)} %dynamic_slice.117, bf16[768,1536]{1,0:T(8,128)(2,1)} %bitcast.136, bf16[512,768]{1,0:T(8,128)(2,1)} %collective-permute-done.4, bf16[512,768]{1,0:T(8,128)(2,1)} %fusion.51), kind=kOutput, calls=%fused_computation.10 | convolution fusion | flops 2453667840 | bytes 13375488 | tf_op jit(solution)/shard_map/dot_general | solution.py:26
  177.3 2.3 collective-permute-done.8
  179.6 1.7 fusion.99
  184.4 2.5 convert_reduce_fusion.4
  192.2 10.3 %convert_reduce_fusion = (f32[1536]{0:T(1024)}, bf16[1024,1536]{1,0:T(8,128)(2,1)S(1)}) fusion(f32[1024,1536]{1,0:T(8,128)} %get-tuple-element.132, f32[1536]{0:T(1024)} %copy-done.52, bf16[768,1536]{1,0:T(8,128)(2,1)} %bitcast.141, bf16[512,768]{1,0:T(8,128)(2,1)} %collective-permute-done.9, bf16[512,768]{1,0:T(8,128)(2,1)} %get-tuple-element.87), kind=kOutput, calls=%fused_computation.8 | convolution fusion | flops 2464676352 | bytes 13381632 | tf_op jit(solution)/shard_map/dot_general | solution.py:26
  204.5 4.6 %convolution_convert_fusion = bf16[768,1536]{1,0:T(8,128)(2,1)S(1)} fusion(bf16[1024,1536]{1,0:T(8,128)(2,1)S(1)} %copy-done.60, bf16[512,768]{1,0:T(8,128)(2,1)} %collective-permute-done.9, bf16[512,768]{1,0:T(8,128)(2,1)} %get-tuple-element.87), kind=kOutput, calls=%fused_computation.12 | convolution fusion | flops 2420244480 | bytes 7077888 | tf_op jit(solution)/shard_map/dot_general | solution.py:30
  213.2 2.7 multiply_reduce_fusion
  216.0 2.3 convert_reduce_fusion.5
  218.2 2.4 convolution_convert_fusion.2
  222.2 5.3 %convolution_convert_fusion.1 = bf16[768,1536]{1,0:T(8,128)(2,1)} fusion(bf16[1024,1536]{1,0:T(8,128)(2,1)S(1)} %get-tuple-element.137, bf16[512,768]{1,0:T(8,128)(2,1)} %collective-permute-done.4, bf16[512,768]{1,0:T(8,128)(2,1)} %fusion.51), kind=kOutput, calls=%fused_computation.13 | convolution fusion | flops 2420244480 | bytes 7077888 | tf_op jit(solution)/shard_map/dot_general | solution.py:30
  234.2 2.1 constant_dynamic-slice_fusion.3
  237.5 18.0 %attend_back.1 = (bf16[1024,384]{1,0:T(8,128)(2,1)S(1)}, bf16[1024,384]{1,0:T(8,128)(2,1)S(1)}, bf16[1024,384]{1,0:T(8,128)(2,1)S(1)}) custom-call(bf16[1024,1152]{1,0:T(8,128)(2,1)S(1)} %multiply_convert_fusion.2.q_ref.k_ref.v_ref, bf16[1024,1152]{1,0:T(8,128)(2,1)S(1)} %multiply_convert_fusion.2.q_ref.k_ref.v_ref, ...), custom_call_target="tpu_custom_call" | custom-call | flops 16106127360 | bytes 9437184 | tf_op jit(solution)/shard_map/attend_back/pallas_call | solution.py:434
  257.5 2.2 fusion.38
  263.8 3.5 pad_dynamic-slice_fusion.1
  267.4 2.6 fusion.14
  270.0 4.9 %all-to-all-start.5 = ((bf16[4,96,1536]{2,1,0:T(8,128)(2,1)}), bf16[4,96,1536]{2,1,0:T(8,128)(2,1)S(1)}, u32[]{:S(2)}, u32[]{:S(2)}) async-start(bf16[4,96,1536]{2,1,0:T(8,128)(2,1)} %fusion.14), calls=%async_computation.5 | async-start | bytes 2359296 | tf_op jit(solution)/shard_map/all_to_all | solution.py:483
  274.9 2.6 fusion.52
  279.6 1.7 add_bitcast_fusion
  281.3 4.4 %fusion.6 = bf16[768,640]{1,0:T(8,128)(2,1)S(1)} fusion(bf16[1024,768]{1,0:T(8,128)(2,1)} %collective-permute-done.13, bf16[1024,768]{1,0:T(8,128)(2,1)S(1)} %copy-done.29, bf16[1024,640]{1,0:T(8,128)(2,1)} %collective-permute-done.14, bf16[1024,640]{1,0:T(8,128)(2,1)S(1)} %copy-done.30), kind=kOutput, calls=%fused_computation.15 | convolution fusion | flops 2024800256 | bytes 6750208 | tf_op jit(solution)/shard_map/dot_general | solution.py:30
  286.9 2.4 slice.281
  290.7 33.4 %collective-permute-done.16 = bf16[4,96,640]{2,1,0:T(8,128)(2,1)S(1)} collective-permute-done((bf16[4,96,640]{2,1,0:T(8,128)(2,1)S(1)}, bf16[4,96,640]{2,1,0:T(8,128)(2,1)S(1)}, u32[]{:S(2)}, u32[]{:S(2)}) %collective-permute-start.16) | collective-permute-done | bytes 491552 | tf_op jit(solution)/shard_map/ppermute | solution.py:479
  325.0 4.8 %all-to-all-start.3 = ((bf16[4,96,640]{2,1,0:T(8,128)(2,1)}), bf16[4,96,640]{2,1,0:T(8,128)(2,1)S(1)}, u32[]{:S(2)}, u32[]{:S(2)}) async-start(bf16[4,96,640]{2,1,0:T(8,128)(2,1)} %fusion.58), calls=%async_computation.3 | async-start | bytes 983040 | tf_op jit(solution)/shard_map/all_to_all | solution.py:483
  329.8 3.3 fusion.10
  336.3 6.5 %all-to-all-done.3 = bf16[4,96,640]{2,1,0:T(8,128)(2,1)S(1)} async-done(((bf16[4,96,640]{2,1,0:T(8,128)(2,1)}), bf16[4,96,640]{2,1,0:T(8,128)(2,1)S(1)}, u32[]{:S(2)}, u32[]{:S(2)}) %all-to-all-start.3) | async-done | bytes 491552 | tf_op jit(solution)/shard_map/all_to_all | solution.py:483
  342.8 3.8 all-to-all-start.4
  346.7 2.8 fusion.60
  350.6 1.6 collective-permute-start.17
  352.3 3.3 collective-permute-done.17
  358.8 22.2 %all-to-all-done.4 = bf16[4,96,1920]{2,1,0:T(8,128)(2,1)S(1)} async-done(((bf16[4,96,1920]{2,1,0:T(8,128)(2,1)}), bf16[4,96,1920]{2,1,0:T(8,128)(2,1)S(1)}, u32[]{:S(2)}, u32[]{:S(2)}) %all-to-all-start.4) | async-done | bytes 1474592 | tf_op jit(solution)/shard_map/all_to_all | solution.py:483
  384.9 5.9 %collective-permute-done.22 = bf16[96,1920]{1,0:T(8,128)(2,1)S(1)} collective-permute-done((bf16[96,1920]{1,0:T(8,128)(2,1)S(1)}, bf16[96,1920]{1,0:T(8,128)(2,1)S(1)}, u32[]{:S(2)}, u32[]{:S(2)}) %collective-permute-start.22) | collective-permute-done | bytes 368672 | tf_op jit(solution)/shard_map/ppermute | solution.py:471
  394.7 4.6 %multiply_add_fusion = (f32[48,9216]{1,0:T(8,128)}, f32[48,9216]{1,0:T(8,128)}, f32[48,9216]{1,0:T(8,128)}, f32[48,9216]{1,0:T(8,128)}) fusion(f32[48,9216]{1,0:T(8,128)S(1)} %copy-done.27, f32[48,9216]{1,0:T(8,128)S(1)} %copy-done.12, f32[48,9216]{1,0:T(8,128)S(1)} %copy-done.28, bf16[48,9216]{1,0:T(8,128)(2,1)} %constant_dynamic-update-slice_fusion.4), kind=kLoop, calls=%fused_computation.41 | loop fusion | flops 5308416 | bytes 13271040 | tf_op jit(solution)/shard_map/add | solution.py:739
  (295 shorter events, 76.1 us)
Async XLA Ops:
  28.8 18.1 %collective-permute-start.1 = (bf16[4,48,2048]{2,1,0:T(8,128)(2,1)S(1)}, bf16[4,48,2048]{2,1,0:T(8,128)(2,1)S(1)}, u32[]{:S(2)}, u32[]{:S(2)}) collective-permute-start(bf16[4,48,2048]{2,1,0:T(8,128)(2,1)S(1)} %all_to_all.30), channel_id=1, source_target_pairs={{0,4},{2,6},{4,0},{6,2},{8,12},{10,14},{12,8},{14,10},{16,20},{18,... | collective-permute-start | bytes 2359304 | tf_op jit(solution)/shard_map/ppermute | solution.py:479
  30.3 28.6 %collective-permute-start = (bf16[512,768]{1,0:T(8,128)(2,1)}, bf16[512,768]{1,0:T(8,128)(2,1)}, u32[]{:S(2)}, u32[]{:S(2)}) collective-permute-start(bf16[512,768]{1,0:T(8,128)(2,1)} %bitcast.151), channel_id=1, source_target_pairs={{0,1},{1,0},{2,3},{3,2},{4,5},{5,4},{6,7},{7,6},{8,9},{9,8},{10,11... | collective-permute-start | bytes 2359304 | tf_op jit(solution)/shard_map/ppermute | solution.py:471
  35.5 13.2 %collective-permute-start.5 = (bf16[48,2,1536]{2,0,1:T(8,128)(2,1)S(1)}, bf16[48,2,1536]{2,0,1:T(8,128)(2,1)S(1)}, u32[]{:S(2)}, u32[]{:S(2)}) collective-permute-start(bf16[48,2,1536]{2,0,1:T(8,128)(2,1)S(1)} %bitcast.159), channel_id=1, source_target_pairs={{0,2},{2,0},{4,6},{6,4},{8,10},{10,8},{12,14},{14,12},{16,18},{18,... | collective-permute-start | bytes 884744 | tf_op jit(solution)/shard_map/ppermute | solution.py:475
  48.3 5.4 %collective-permute-start.2 = (bf16[4,2,48,2048]{3,2,0,1:T(8,128)(2,1)}, bf16[4,2,48,2048]{3,2,0,1:T(8,128)(2,1)}, u32[]{:S(2)}, u32[]{:S(2)}) collective-permute-start(bf16[4,2,48,2048]{3,2,0,1:T(8,128)(2,1)} %maximum_select_fusion.4), channel_id=1, source_target_pairs={{0,2},{2,0},{4,6},{6,4},{8,10},{10,8},{12,14},{14,12},{16,18},{18,... | collective-permute-start | bytes 4718600 | tf_op jit(solution)/shard_map/ppermute | solution.py:475
  50.0 33.0 %all-to-all-start.1 = ((bf16[4,96,1536]{2,1,0:T(8,128)(2,1)}), bf16[4,96,1536]{2,1,0:T(8,128)(2,1)S(1)}, u32[]{:S(2)}, u32[]{:S(2)}) async-start(bf16[4,96,1536]{2,1,0:T(8,128)(2,1)} %broadcast_in_dim.118), calls=%async_computation.1 | async-start | bytes 2359296 | tf_op jit(solution)/shard_map/all_to_all | solution.py:483
  84.4 33.6 %all-to-all-start.2 = ((bf16[4,96,1536]{2,1,0:T(8,128)(2,1)}), bf16[4,96,1536]{2,1,0:T(8,128)(2,1)}, u32[]{:S(2)}, u32[]{:S(2)}) async-start(bf16[4,96,1536]{2,1,0:T(8,128)(2,1)} %broadcast_in_dim.122), calls=%async_computation.2 | async-start | bytes 2359296 | tf_op jit(solution)/shard_map/all_to_all | solution.py:483
  105.0 14.4 %collective-permute-start.3 = (bf16[512,384]{1,0:T(8,128)(2,1)}, bf16[512,384]{1,0:T(8,128)(2,1)}, u32[]{:S(2)}, u32[]{:S(2)}) collective-permute-start(bf16[512,384]{1,0:T(8,128)(2,1)} %get-tuple-element.102), channel_id=1, source_target_pairs={{0,1},{1,0},{2,3},{3,2},{4,5},{5,4},{6,7},{7,6},{8,9},{9,8},{10,11... | collective-permute-start | bytes 1179656 | tf_op jit(solution)/shard_map/ppermute | solution.py:471
  106.5 29.2 %collective-permute-start.6 = (bf16[4,96,1536]{2,1,0:T(8,128)(2,1)}, bf16[4,96,1536]{2,1,0:T(8,128)(2,1)}, u32[]{:S(2)}, u32[]{:S(2)}) collective-permute-start(bf16[4,96,1536]{2,1,0:T(8,128)(2,1)} %copy-done.17), channel_id=1, source_target_pairs={{0,4},{2,6},{4,0},{6,2},{8,12},{10,14},{12,8},{14,10},{16,20},{18,... | collective-permute-start | bytes 3538952 | tf_op jit(solution)/shard_map/ppermute | solution.py:479
  118.0 41.5 %collective-permute-start.7 = (bf16[4,96,1536]{2,1,0:T(8,128)(2,1)}, bf16[4,96,1536]{2,1,0:T(8,128)(2,1)}, u32[]{:S(2)}, u32[]{:S(2)}) collective-permute-start(bf16[4,96,1536]{2,1,0:T(8,128)(2,1)} %all-to-all-done.2), channel_id=1, source_target_pairs={{0,4},{2,6},{4,0},{6,2},{8,12},{10,14},{12,8},{14,10},{16,20},{18,... | collective-permute-start | bytes 3538952 | tf_op jit(solution)/shard_map/ppermute | solution.py:479
  124.4 55.3 %copy-start.38 = (f32[512]{0:T(512)}, f32[512]{0:T(512)S(1)}, u32[]{:S(2)}) copy-start(f32[512]{0:T(512)S(1)} %add_rsqrt_fusion.1) | copy-start | bytes 6148
  125.6 40.3 %collective-permute-start.4 = (bf16[512,768]{1,0:T(8,128)(2,1)}, bf16[512,768]{1,0:T(8,128)(2,1)}, u32[]{:S(2)}, u32[]{:S(2)}) collective-permute-start(bf16[512,768]{1,0:T(8,128)(2,1)} %fusion.51), channel_id=1, source_target_pairs={{0,2},{2,0},{4,6},{6,4},{8,10},{10,8},{12,14},{14,12},{16,18},{18,... | collective-permute-start | bytes 2359304 | tf_op jit(solution)/shard_map/ppermute | solution.py:475
  165.9 9.9 %copy-start.52 = (f32[1536]{0:T(1024)}, f32[1536]{0:T(1024)S(1)}, u32[]{:S(2)}) copy-start(f32[1536]{0:T(1024)S(1)} %dynamic_slice.117) | copy-start | bytes 18436
  165.9 9.9 %copy-start.25 = (bf16[4,2,96,1536]{3,2,1,0:T(8,128)(2,1)S(1)}, bf16[4,2,96,1536]{3,2,1,0:T(8,128)(2,1)}, u32[]{:S(2)}) copy-start(bf16[4,2,96,1536]{3,2,1,0:T(8,128)(2,1)} %maximum_select_fusion.2) | copy-start | bytes 7077892
  177.3 2.4 collective-permute-start.8
  181.7 5.2 %copy-start.40 = (f32[512]{0:T(512)}, f32[512]{0:T(512)S(1)}, u32[]{:S(2)}) copy-start(f32[512]{0:T(512)S(1)} %add_rsqrt_fusion) | copy-start | bytes 6148
  186.9 5.4 %collective-permute-start.9 = (bf16[512,768]{1,0:T(8,128)(2,1)}, bf16[512,768]{1,0:T(8,128)(2,1)}, u32[]{:S(2)}, u32[]{:S(2)}) collective-permute-start(bf16[512,768]{1,0:T(8,128)(2,1)} %get-tuple-element.87), channel_id=1, source_target_pairs={{0,2},{2,0},{4,6},{6,4},{8,10},{10,8},{12,14},{14,12},{16,18},{18,... | collective-permute-start | bytes 2359304 | tf_op jit(solution)/shard_map/ppermute | solution.py:475
  189.1 92.2 %collective-permute-start.13 = (bf16[1024,768]{1,0:T(8,128)(2,1)}, bf16[1024,768]{1,0:T(8,128)(2,1)}, u32[]{:S(2)}, u32[]{:S(2)}) collective-permute-start(bf16[1024,768]{1,0:T(8,128)(2,1)} %get-tuple-element.127), channel_id=1, source_target_pairs={{0,2},{2,0},{4,6},{6,4},{8,10},{10,8},{12,14},{14,12},{16,18},{18,... | collective-permute-start | bytes 4718600 | tf_op jit(solution)/shard_map/ppermute | solution.py:475
  189.6 85.3 %collective-permute-start.19 = (bf16[512,768]{1,0:T(8,128)(2,1)}, bf16[512,768]{1,0:T(8,128)(2,1)}, u32[]{:S(2)}, u32[]{:S(2)}) collective-permute-start(bf16[512,768]{1,0:T(8,128)(2,1)} %copy-done.31), channel_id=1, source_target_pairs={{0,2},{2,0},{4,6},{6,4},{8,10},{10,8},{12,14},{14,12},{16,18},{18,... | collective-permute-start | bytes 2359304 | tf_op jit(solution)/shard_map/ppermute | solution.py:475
  192.2 10.3 %copy-start.22 = (bf16[4,2,96,1536]{3,2,1,0:T(8,128)(2,1)S(1)}, bf16[4,2,96,1536]{3,2,1,0:T(8,128)(2,1)}, u32[]{:S(2)}) copy-start(bf16[4,2,96,1536]{3,2,1,0:T(8,128)(2,1)} %maximum_select_fusion.1) | copy-start | bytes 7077892
  204.0 9.1 %collective-permute-start.10 = (bf16[512,768]{1,0:T(8,128)(2,1)S(1)}, bf16[512,768]{1,0:T(8,128)(2,1)S(1)}, u32[]{:S(2)}, u32[]{:S(2)}) collective-permute-start(bf16[512,768]{1,0:T(8,128)(2,1)S(1)} %fusion.48), channel_id=1, source_target_pairs={{0,2},{2,0},{4,6},{6,4},{8,10},{10,8},{12,14},{14,12},{16,18},{18,... | collective-permute-start | bytes 2359304 | tf_op jit(solution)/shard_map/ppermute | solution.py:475
  204.5 8.7 %copy-start.8 = (f32[512,768]{1,0:T(8,128)S(1)}, f32[512,768]{1,0:T(8,128)}, u32[]{:S(2)}) copy-start(f32[512,768]{1,0:T(8,128)} %copy-done.7) | copy-start | bytes 4718596
  204.5 8.7 %copy-start.39 = (f32[512]{0:T(512)S(1)}, f32[512]{0:T(512)}, u32[]{:S(2)}) copy-start(f32[512]{0:T(512)} %copy-done.38) | copy-start | bytes 6148
  204.5 8.7 %copy-start.41 = (f32[512]{0:T(512)S(1)}, f32[512]{0:T(512)}, u32[]{:S(2)}) copy-start(f32[512]{0:T(512)} %copy-done.40) | copy-start | bytes 6148
  204.5 8.7 %copy-start.49 = (f32[512]{0:T(512)S(1)}, f32[512]{0:T(512)}, u32[]{:S(2)}) copy-start(f32[512]{0:T(512)} %copy-done.48) | copy-start | bytes 6148
  204.5 8.7 %copy-start.51 = (f32[512]{0:T(512)S(1)}, f32[512]{0:T(512)}, u32[]{:S(2)}) copy-start(f32[512]{0:T(512)} %copy-done.50) | copy-start | bytes 6148
  211.7 55.6 %collective-permute-start.24 = (bf16[4,96,1536]{2,1,0:T(8,128)(2,1)}, bf16[4,96,1536]{2,1,0:T(8,128)(2,1)}, u32[]{:S(2)}, u32[]{:S(2)}) collective-permute-start(bf16[4,96,1536]{2,1,0:T(8,128)(2,1)} %dynamic-slice_bitcast_fusion.1), channel_id=1, source_target_pairs={{0,4},{2,6},{4,0},{6,2},{8,12},{10,14},{12,8},{14,10},{16,20},{18,... | collective-permute-start | bytes 3538952 | tf_op jit(solution)/shard_map/ppermute | solution.py:479
  221.6 6.5 %copy-start.53 = (f32[1536]{0:T(1024)S(1)}, f32[1536]{0:T(1024)}, u32[]{:S(2)}) copy-start(f32[1536]{0:T(1024)} %get-tuple-element.136) | copy-start | bytes 18436
  221.6 14.7 %collective-permute-start.11 = (bf16[512,384]{1,0:T(8,128)(2,1)}, bf16[512,384]{1,0:T(8,128)(2,1)}, u32[]{:S(2)}, u32[]{:S(2)}) collective-permute-start(bf16[512,384]{1,0:T(8,128)(2,1)} %get-tuple-element.100), channel_id=1, source_target_pairs={{0,1},{1,0},{2,3},{3,2},{4,5},{5,4},{6,7},{7,6},{8,9},{9,8},{10,11... | collective-permute-start | bytes 1179656 | tf_op jit(solution)/shard_map/ppermute | solution.py:471
  230.3 7.2 %copy-start.1 = (f32[1024,384]{1,0:T(8,128)S(1)}, f32[1024,384]{1,0:T(8,128)}, u32[]{:S(2)}) copy-start(f32[1024,384]{1,0:T(8,128)} %copy-done) | copy-start | bytes 4718596
  236.3 38.6 %collective-permute-start.20 = (bf16[512,384]{1,0:T(8,128)(2,1)}, bf16[512,384]{1,0:T(8,128)(2,1)}, u32[]{:S(2)}, u32[]{:S(2)}) collective-permute-start(bf16[512,384]{1,0:T(8,128)(2,1)} %get-tuple-element.98), channel_id=1, source_target_pairs={{0,2},{2,0},{4,6},{6,4},{8,10},{10,8},{12,14},{14,12},{16,18},{18,... | collective-permute-start | bytes 1179656 | tf_op jit(solution)/shard_map/ppermute | solution.py:475
  263.3 16.3 %collective-permute-start.15 = (f32[16,768]{0,1:T(8,128)S(1)}, f32[16,768]{0,1:T(8,128)}, u32[]{:S(2)}, u32[]{:S(2)}) collective-permute-start(f32[16,768]{0,1:T(8,128)S(1)} %copy.173), channel_id=1, source_target_pairs={{0,2},{2,0},{4,6},{6,4},{8,10},{10,8},{12,14},{14,12},{16,18},{18,... | collective-permute-start | bytes 147464 | tf_op jit(solution)/shard_map/ppermute | solution.py:475
  267.3 14.0 %collective-permute-start.14 = (bf16[1024,640]{1,0:T(8,128)(2,1)}, bf16[1024,640]{1,0:T(8,128)(2,1)}, u32[]{:S(2)}, u32[]{:S(2)}) collective-permute-start(bf16[1024,640]{1,0:T(8,128)(2,1)} %get-tuple-element.92), channel_id=1, source_target_pairs={{0,2},{2,0},{4,6},{6,4},{8,10},{10,8},{12,14},{14,12},{16,18},{18,... | collective-permute-start | bytes 3932168 | tf_op jit(solution)/shard_map/ppermute | solution.py:475
  270.0 55.1 %all-to-all-start.5 = ((bf16[4,96,1536]{2,1,0:T(8,128)(2,1)}), bf16[4,96,1536]{2,1,0:T(8,128)(2,1)S(1)}, u32[]{:S(2)}, u32[]{:S(2)}) async-start(bf16[4,96,1536]{2,1,0:T(8,128)(2,1)} %fusion.14), calls=%async_computation.5 | async-start | bytes 2359296 | tf_op jit(solution)/shard_map/all_to_all | solution.py:483
  279.0 50.8 %collective-permute-start.21 = (bf16[4,96,1920]{2,1,0:T(8,128)(2,1)}, bf16[4,96,1920]{2,1,0:T(8,128)(2,1)}, u32[]{:S(2)}, u32[]{:S(2)}) collective-permute-start(bf16[4,96,1920]{2,1,0:T(8,128)(2,1)} %dynamic-slice_bitcast_fusion), channel_id=1, source_target_pairs={{0,4},{2,6},{4,0},{6,2},{8,12},{10,14},{12,8},{14,10},{16,20},{18,... | collective-permute-start | bytes 4423688 | tf_op jit(solution)/shard_map/ppermute | solution.py:479
  286.0 38.1 %collective-permute-start.16 = (bf16[4,96,640]{2,1,0:T(8,128)(2,1)S(1)}, bf16[4,96,640]{2,1,0:T(8,128)(2,1)S(1)}, u32[]{:S(2)}, u32[]{:S(2)}) collective-permute-start(bf16[4,96,640]{2,1,0:T(8,128)(2,1)S(1)} %fusion.65), channel_id=1, source_target_pairs={{0,4},{2,6},{4,0},{6,2},{8,12},{10,14},{12,8},{14,10},{16,20},{18,... | collective-permute-start | bytes 1474568 | tf_op jit(solution)/shard_map/ppermute | solution.py:479
  289.2 57.4 %collective-permute-start.12 = (bf16[512,768]{1,0:T(8,128)(2,1)}, bf16[512,768]{1,0:T(8,128)(2,1)}, u32[]{:S(2)}, u32[]{:S(2)}) collective-permute-start(bf16[512,768]{1,0:T(8,128)(2,1)} %slice.281), channel_id=1, source_target_pairs={{0,1},{1,0},{2,3},{3,2},{4,5},{5,4},{6,7},{7,6},{8,9},{9,8},{10,11... | collective-permute-start | bytes 2359304 | tf_op jit(solution)/shard_map/ppermute | solution.py:471
  325.0 17.8 %all-to-all-start.3 = ((bf16[4,96,640]{2,1,0:T(8,128)(2,1)}), bf16[4,96,640]{2,1,0:T(8,128)(2,1)S(1)}, u32[]{:S(2)}, u32[]{:S(2)}) async-start(bf16[4,96,640]{2,1,0:T(8,128)(2,1)} %fusion.58), calls=%async_computation.3 | async-start | bytes 983040 | tf_op jit(solution)/shard_map/all_to_all | solution.py:483
  334.8 14.7 %collective-permute-start.25 = (bf16[96,1536]{1,0:T(8,128)(2,1)}, bf16[96,1536]{1,0:T(8,128)(2,1)}, u32[]{:S(2)}, u32[]{:S(2)}) collective-permute-start(bf16[96,1536]{1,0:T(8,128)(2,1)} %convert_element_type.228), channel_id=1, source_target_pairs={{0,1},{1,0},{2,3},{3,2},{4,5},{5,4},{6,7},{7,6},{8,9},{9,8},{10,11... | collective-permute-start | bytes 884744 | tf_op jit(solution)/shard_map/ppermute | solution.py:471
  342.8 38.2 %all-to-all-start.4 = ((bf16[4,96,1920]{2,1,0:T(8,128)(2,1)}), bf16[4,96,1920]{2,1,0:T(8,128)(2,1)S(1)}, u32[]{:S(2)}, u32[]{:S(2)}) async-start(bf16[4,96,1920]{2,1,0:T(8,128)(2,1)} %fusion.10), calls=%async_computation.4 | async-start | bytes 2949120 | tf_op jit(solution)/shard_map/all_to_all | solution.py:483
  350.6 4.9 %collective-permute-start.17 = (bf16[96,640]{1,0:T(8,128)(2,1)S(1)}, bf16[96,640]{1,0:T(8,128)(2,1)S(1)}, u32[]{:S(2)}, u32[]{:S(2)}) collective-permute-start(bf16[96,640]{1,0:T(8,128)(2,1)S(1)} %reduce_sum.200), channel_id=1, source_target_pairs={{0,1},{1,0},{2,3},{3,2},{4,5},{5,4},{6,7},{7,6},{8,9},{9,8},{10,11... | collective-permute-start | bytes 368648 | tf_op jit(solution)/shard_map/ppermute | solution.py:471
  352.2 3.5 collective-permute-start.26
  355.6 1.4 collective-permute-start.18
  358.8 25.5 %copy-start.37 = (f32[48,15]{0,1:T(8,128)S(1)}, f32[48,15]{0,1:T(8,128)}, u32[]{:S(2)}) copy-start(f32[48,15]{0,1:T(8,128)} %param.17) | copy-start | bytes 8644
  358.8 25.5 %copy-start.54 = (f32[48,15]{0,1:T(8,128)S(1)}, f32[48,15]{0,1:T(8,128)}, u32[]{:S(2)}) copy-start(f32[48,15]{0,1:T(8,128)} %param.19) | copy-start | bytes 8644
  358.8 25.5 %copy-start.55 = (f32[48,15]{0,1:T(8,128)S(1)}, f32[48,15]{0,1:T(8,128)}, u32[]{:S(2)}) copy-start(f32[48,15]{0,1:T(8,128)} %param.18) | copy-start | bytes 8644
  381.2 9.6 %collective-permute-start.22 = (bf16[96,1920]{1,0:T(8,128)(2,1)S(1)}, bf16[96,1920]{1,0:T(8,128)(2,1)S(1)}, u32[]{:S(2)}, u32[]{:S(2)}) collective-permute-start(bf16[96,1920]{1,0:T(8,128)(2,1)S(1)} %convert_element_type.219), channel_id=1, source_target_pairs={{0,1},{1,0},{2,3},{3,2},{4,5},{5,4},{6,7},{7,6},{8,9},{9,8},{10,11... | collective-permute-start | bytes 1105928 | tf_op jit(solution)/shard_map/ppermute | solution.py:471
  384.9 7.7 %copy-start.56 = (f32[48,15]{0,1:T(8,128)}, f32[48,15]{0,1:T(8,128)S(1)}, u32[]{:S(2)}) copy-start(f32[48,15]{0,1:T(8,128)S(1)} %get-tuple-element.81) | copy-start | bytes 8644
  390.9 1.5 collective-permute-start.23
  (45 other events, 118.7 us)
